TPU v7x, 32 devices: a whole 2x2x4 slice. The times are simulated.
32 devices in a mesh: grp: 2 (over y), col: 4 (over z), lev: 4 (over x, core).
Axes of the slice: x: 2, y: 2, z: 4, core: 2. Of those that a mesh axis runs over, the one named last changes fastest.
Arguments:
- control: float32 [256, 32, 256], P(('grp', 'lev'), 'col'), parts along dimension 0, may hold values from -6 to 6
- control_ens: float32 [4, 128, 32, 256], P('grp', 'lev', 'col'), parts along dimension 0, may hold values from -6 to 6
- ensemble: bfloat16 [4, 128, 32, 256], P('grp', 'lev', 'col'), parts along dimension 0, may hold values from -6 to 6
- spread: float32 [256, 32, 256], P(('grp', 'lev'), 'col'), parts along dimension 0, may hold values from 0.3 to 3
- jacobian: bfloat16 [128, 128, 128], P(('grp', 'col'), 'lev'), parts along dimension 0, may hold values from -0.5 to 0.5
- obs_value: bfloat16 [128, 128], P(('grp', 'col')), parts along dimension 0, may hold values from -6 to 6
- obs_weight: bfloat16 [128, 128], P(('grp', 'col')), parts along dimension 0, may hold values from 1 to 10
- channel_mask: int32 [128, 128], P(('grp', 'col')), parts along dimension 0, may hold values 0 or 1
- obs_cell: int32 [128], P(('grp', 'col')), parts along dimension 0, may hold values from 0 to 2047
- obs_count: int32 [8, 4], P(('grp', 'col')), parts along dimension 0, may hold values from 1 to 4, as said below
Outputs:
- grad_control: float32 [256, 32, 256], P(('grp', 'lev'), 'col'), parts along dimension 0
- grad_ens: float32 [4, 128, 32, 256], P('grp', 'lev', 'col'), parts along dimension 0
- departures: float32 [128, 128], P(('grp', 'col')), parts along dimension 0
There are 2 independent parts, one for each index of `grp`. A program takes and returns all parts, laid end to end along the dimension named above; each array names one. Nothing has to cross between parts.
Inputs may be any that keep to these rules, and one draw needn't show every extreme that they name: `obs_count`: for every sending block some target gets exactly 4 filled slots, and one target gets 4 from every sending block.
All inputs are finite; a program needn't handle non-finite values. No bound on the sum of `channel_mask` on one device may be relied on, other than what follows from the above.
Results may differ from a plain program's by a relative error of at most 0.0013.
Values may be sent and summed in bfloat16 or wider, within the bound.
A program may use at most 64 MiB of HBM per device.

v0:
```python
import math

import jax
import jax.numpy as jnp
from jax import lax
from jax.sharding import PartitionSpec as P

STEPS = 4


rate_x = 0.35
rate_y = 0.1


def padded_2(value, sides, width):
    for axis, dim in sides:
        peers, length = (lax.axis_size(axis), value.shape[dim])
        up = [(i, (i + 1) % peers) for i in range(peers)]
        down = [(j, i) for i, j in up]
        last = lax.slice_in_dim(value, length - width, length, axis=dim)
        initial = lax.slice_in_dim(value, 0, width, axis=dim)
        before = lax.ppermute(last, axis, up)
        after = lax.ppermute(initial, axis, down)
        value = jnp.concatenate([before, value, after], axis=dim)
    return value


def smooth(fields):
    for iteration in range(STEPS):
        padded = padded_2(fields, (("col", 2),), 1)
        beside = jnp.pad(fields, ((0, 0), (0, 0), (0, 0), (1, 1)))
        along_x = padded[:, :, 2:, :] + padded[:, :, :-2, :] - 2.0 * fields
        along_y = beside[..., 2:] + beside[..., :-2] - 2.0 * fields
        fields = fields + rate_x * along_x + rate_y * along_y
    return fields


def solve_rows(jac_rows, columns, values, weights, masks, filled):
    partial_value = jnp.einsum("rlc,rl->rc", jac_rows, columns, preferred_element_type=jnp.float32)
    radiance = lax.psum(partial_value, "lev")
    active = (filled[:, None] > 0) & (masks > 0)
    departure = jnp.where(
        active, weights.astype(jnp.float32) * (radiance - values.astype(jnp.float32)), 0.0
    )
    increment = jnp.einsum(
        "rc,rlc->rl", departure.astype(jnp.bfloat16), jac_rows, preferred_element_type=jnp.float32
    )
    return (departure, increment)


def local(
    control,
    control_ens,
    ensemble,
    spread,
    jacobian,
    obs_value,
    obs_weight,
    channel_mask,
    obs_cell,
    obs_count,
):
    members = control_ens.shape[0]
    ens_scale = 1.0 / math.sqrt(members)
    levels, cells_x, cells_y = control.shape
    peer_count = lax.axis_size("col")
    slot_total = jacobian.shape[0]
    capacity = slot_total // peer_count
    smoothed = smooth(jnp.concatenate([control[None], control_ens], 0))
    analysis = spread * smoothed[0] + jnp.sum(ensemble * smoothed[1:], 0) * ens_scale
    flat_state = analysis.reshape(levels, cells_x * cells_y)
    row_ids = jnp.arange(slot_total, dtype=jnp.int32)
    target = row_ids // capacity
    slot_index = row_ids % capacity
    filled = (slot_index < obs_count[0][target]).astype(jnp.int32)
    empty_grid = jnp.zeros((levels, cells_x * cells_y), jnp.float32)
    jac_recv, value_recv, weight_recv, mask_recv, cell_recv, filled_recv = (
        lax.all_to_all(jacobian, "col", split_axis=0, concat_axis=0, tiled=True),
        lax.all_to_all(obs_value, "col", split_axis=0, concat_axis=0, tiled=True),
        lax.all_to_all(obs_weight, "col", split_axis=0, concat_axis=0, tiled=True),
        lax.all_to_all(channel_mask, "col", split_axis=0, concat_axis=0, tiled=True),
        lax.all_to_all(obs_cell, "col", split_axis=0, concat_axis=0, tiled=True),
        lax.all_to_all(filled, "col", split_axis=0, concat_axis=0, tiled=True),
    )
    columns = flat_state[:, cell_recv].T.astype(jnp.bfloat16)
    departure, increment = solve_rows(
        jac_recv, columns, value_recv, weight_recv, mask_recv, filled_recv
    )
    gradient_flat = empty_grid.at[:, cell_recv].add(increment.T)
    departures = lax.all_to_all(departure, "col", split_axis=0, concat_axis=0, tiled=True)
    gradient_field = gradient_flat.reshape(levels, cells_x, cells_y)
    adjoint = smooth(
        jnp.concatenate(
            [(spread * gradient_field)[None], ensemble * gradient_field[None] * ens_scale], 0
        )
    )
    return (control + adjoint[0], control_ens + adjoint[1:], departures)


def solution(mesh):
    placed = (
        P(("grp", "lev"), "col", None),
        P("grp", "lev", "col", None),
        P("grp", "lev", "col", None),
        P(("grp", "lev"), "col", None),
        P(("grp", "col"), "lev", None),
        P(("grp", "col"), None),
        P(("grp", "col"), None),
        P(("grp", "col"), None),
        P(("grp", "col")),
        P(("grp", "col"), None),
    )
    return jax.shard_map(
        local,
        mesh=mesh,
        in_specs=placed,
        out_specs=(
            P(("grp", "lev"), "col", None),
            P("grp", "lev", "col", None),
            P(("grp", "col"), None),
        ),
        check_vma=False,
    )
```

profile of v0, /device:TPU:0, one launch (start us, length us, event | category | flops | bytes accessed | tf_op | source)
XLA Modules:
  0.0 123.3 jit_solution(3359703883084494433)
XLA Ops:
  2.0 5.1 %collective-permute-start = (f32[3,32,1,256]{3,1,2,0:T(8,128)S(1)}, f32[3,32,1,256]{3,1,2,0:T(8,128)S(1)}, u32[]{:S(2)}, u32[]{:S(2)}) collective-permute-start(f32[3,32,1,256]{3,1,2,0:T(8,128)S(1)} %get-tuple-element.22), channel_id=1, source_target_pairs={{4,0},{8,4},{12,8},{0,12},{5,1},{9,5},{13,9},{1,13},{6,2},{10,6},{... | collective-permute-start | bytes 294920 | tf_op jit(solution)/shard_map/ppermute | solution.py:23
  8.5 5.1 %all-to-all-start.1 = ((s32[4,4,1]{1,2,0:T(1,128)}), s32[4,4,1]{1,2,0:T(1,128)S(1)}, u32[]{:S(2)}, u32[]{:S(2)}) async-start(s32[4,4,1]{1,2,0:T(1,128)} %bitcast.4), calls=%async_computation.1 | async-start | bytes 4096 | tf_op jit(solution)/shard_map/all_to_all | solution.py:83
  14.4 4.7 %all-to-all-done.1 = s32[4,4,1]{1,2,0:T(1,128)S(1)} async-done(((s32[4,4,1]{1,2,0:T(1,128)}), s32[4,4,1]{1,2,0:T(1,128)S(1)}, u32[]{:S(2)}, u32[]{:S(2)}) %all-to-all-start.1) | async-done | bytes 96 | tf_op jit(solution)/shard_map/all_to_all | solution.py:83
  19.1 3.2 %all-to-all-start = ((s32[4,4,1]{1,2,0:T(1,128)}), s32[4,4,1]{1,2,0:T(1,128)S(1)}, u32[]{:S(2)}, u32[]{:S(2)}) async-start(s32[4,4,1]{1,2,0:T(1,128)} %bitcast), calls=%async_computation | async-start | bytes 4096 | tf_op jit(solution)/shard_map/all_to_all | solution.py:82
  22.3 5.4 %all-to-all-done = s32[4,4,1]{1,2,0:T(1,128)S(1)} async-done(((s32[4,4,1]{1,2,0:T(1,128)}), s32[4,4,1]{1,2,0:T(1,128)S(1)}, u32[]{:S(2)}, u32[]{:S(2)}) %all-to-all-start) | async-done | bytes 96 | tf_op jit(solution)/shard_map/all_to_all | solution.py:82
  27.8 3.2 %all-to-all-start.2 = ((s32[4,4,128]{2,1,0:T(4,128)}), s32[4,4,128]{2,1,0:T(4,128)S(1)}, u32[]{:S(2)}, u32[]{:S(2)}) async-start(s32[4,4,128]{2,1,0:T(4,128)} %bitcast.6), calls=%async_computation.2 | async-start | bytes 16384 | tf_op jit(solution)/shard_map/all_to_all | solution.py:81
  32.8 3.8 %collective-permute-start.2 = (f32[3,32,1,256]{3,1,2,0:T(8,128)S(1)}, f32[3,32,1,256]{3,1,2,0:T(8,128)S(1)}, u32[]{:S(2)}, u32[]{:S(2)}) collective-permute-start(f32[3,32,1,256]{3,1,2,0:T(8,128)S(1)} %get-tuple-element.20), channel_id=1, source_target_pairs={{4,0},{8,4},{12,8},{0,12},{5,1},{9,5},{13,9},{1,13},{6,2},{10,6},{... | collective-permute-start | bytes 294920 | tf_op jit(solution)/shard_map/ppermute | solution.py:23
  36.8 2.1 %collective-permute-done.2 = f32[3,32,1,256]{3,1,2,0:T(8,128)S(1)} collective-permute-done((f32[3,32,1,256]{3,1,2,0:T(8,128)S(1)}, f32[3,32,1,256]{3,1,2,0:T(8,128)S(1)}, u32[]{:S(2)}, u32[]{:S(2)}) %collective-permute-start.2) | collective-permute-done | bytes 98336 | tf_op jit(solution)/shard_map/ppermute | solution.py:23
  38.9 4.3 %collective-permute-done.3 = f32[3,32,1,256]{3,1,2,0:T(8,128)S(1)} collective-permute-done((f32[3,32,1,256]{3,1,2,0:T(8,128)S(1)}, f32[3,32,1,256]{3,1,2,0:T(8,128)S(1)}, u32[]{:S(2)}, u32[]{:S(2)}) %collective-permute-start.3) | collective-permute-done | bytes 98336 | tf_op jit(solution)/shard_map/ppermute | solution.py:22
  45.8 3.5 %collective-permute-done.4 = f32[3,32,1,256]{3,1,2,0:T(8,128)S(1)} collective-permute-done((f32[3,32,1,256]{3,1,2,0:T(8,128)S(1)}, f32[3,32,1,256]{3,1,2,0:T(8,128)S(1)}, u32[]{:S(2)}, u32[]{:S(2)}) %collective-permute-start.4) | collective-permute-done | bytes 98336 | tf_op jit(solution)/shard_map/ppermute | solution.py:23
  53.4 3.3 %all-to-all-start.4 = ((bf16[16,32,128]{2,1,0:T(8,128)(2,1)}), bf16[16,32,128]{2,1,0:T(8,128)(2,1)S(1)}, u32[]{:S(2)}, u32[]{:S(2)}) async-start(bf16[16,32,128]{2,1,0:T(8,128)(2,1)} %param.14), calls=%async_computation.4 | async-start | bytes 262144 | tf_op jit(solution)/shard_map/all_to_all | solution.py:78
  59.7 3.0 %all-to-all-done.4 = bf16[16,32,128]{2,1,0:T(8,128)(2,1)S(1)} async-done(((bf16[16,32,128]{2,1,0:T(8,128)(2,1)}), bf16[16,32,128]{2,1,0:T(8,128)(2,1)S(1)}, u32[]{:S(2)}, u32[]{:S(2)}) %all-to-all-start.4) | async-done | bytes 131104 | tf_op jit(solution)/shard_map/all_to_all | solution.py:78
  62.7 3.2 %all-to-all-start.3 = ((bf16[4,4,128]{2,1,0:T(4,128)(2,1)}), bf16[4,4,128]{2,1,0:T(4,128)(2,1)S(1)}, u32[]{:S(2)}, u32[]{:S(2)}) async-start(bf16[4,4,128]{2,1,0:T(4,128)(2,1)} %bitcast.8), calls=%async_computation.3 | async-start | bytes 8192 | tf_op jit(solution)/shard_map/all_to_all | solution.py:80
  66.1 5.4 %all-to-all-done.3 = bf16[4,4,128]{2,1,0:T(4,128)(2,1)S(1)} async-done(((bf16[4,4,128]{2,1,0:T(4,128)(2,1)}), bf16[4,4,128]{2,1,0:T(4,128)(2,1)S(1)}, u32[]{:S(2)}, u32[]{:S(2)}) %all-to-all-start.3) | async-done | bytes 4128 | tf_op jit(solution)/shard_map/all_to_all | solution.py:80
  71.5 3.2 %all-to-all-start.5 = ((bf16[4,4,128]{2,1,0:T(4,128)(2,1)}), bf16[4,4,128]{2,1,0:T(4,128)(2,1)S(1)}, u32[]{:S(2)}, u32[]{:S(2)}) async-start(bf16[4,4,128]{2,1,0:T(4,128)(2,1)} %bitcast.16), calls=%async_computation.5 | async-start | bytes 8192 | tf_op jit(solution)/shard_map/all_to_all | solution.py:79
  74.7 5.8 %psum.7 = f32[16,128]{1,0:T(8,128)S(1)} all-reduce(f32[16,128]{1,0:T(8,128)S(1)} %bitcast.61), channel_id=1, replica_groups=mesh['grp'=2,'col'=4,'lev'=4] {'lev'}, use_global_device_ids=true, to_apply=%region_1.2 | all-reduce | flops 2048 | bytes 16384 | tf_op jit(solution)/shard_map/psum | solution.py:40
  82.2 3.8 %collective-permute-start.8 = (f32[3,32,1,256]{3,1,2,0:T(8,128)S(1)}, f32[3,32,1,256]{3,1,2,0:T(8,128)S(1)}, u32[]{:S(2)}, u32[]{:S(2)}) collective-permute-start(f32[3,32,1,256]{3,1,2,0:T(8,128)S(1)} %get-tuple-element.14), channel_id=1, source_target_pairs={{4,0},{8,4},{12,8},{0,12},{5,1},{9,5},{13,9},{1,13},{6,2},{10,6},{... | collective-permute-start | bytes 294920 | tf_op jit(solution)/shard_map/ppermute | solution.py:23
  86.1 3.1 %collective-permute-done.8 = f32[3,32,1,256]{3,1,2,0:T(8,128)S(1)} collective-permute-done((f32[3,32,1,256]{3,1,2,0:T(8,128)S(1)}, f32[3,32,1,256]{3,1,2,0:T(8,128)S(1)}, u32[]{:S(2)}, u32[]{:S(2)}) %collective-permute-start.8) | collective-permute-done | bytes 98336 | tf_op jit(solution)/shard_map/ppermute | solution.py:23
  89.2 3.2 %collective-permute-done.9 = f32[3,32,1,256]{3,1,2,0:T(8,128)S(1)} collective-permute-done((f32[3,32,1,256]{3,1,2,0:T(8,128)S(1)}, f32[3,32,1,256]{3,1,2,0:T(8,128)S(1)}, u32[]{:S(2)}, u32[]{:S(2)}) %collective-permute-start.9) | collective-permute-done | bytes 98336 | tf_op jit(solution)/shard_map/ppermute | solution.py:22
  95.1 3.3 %collective-permute-done.10 = f32[3,32,1,256]{3,1,2,0:T(8,128)S(1)} collective-permute-done((f32[3,32,1,256]{3,1,2,0:T(8,128)S(1)}, f32[3,32,1,256]{3,1,2,0:T(8,128)S(1)}, u32[]{:S(2)}, u32[]{:S(2)}) %collective-permute-start.10) | collective-permute-done | bytes 98336 | tf_op jit(solution)/shard_map/ppermute | solution.py:23
  98.4 2.4 %collective-permute-done.11 = f32[3,32,1,256]{3,1,2,0:T(8,128)S(1)} collective-permute-done((f32[3,32,1,256]{3,1,2,0:T(8,128)S(1)}, f32[3,32,1,256]{3,1,2,0:T(8,128)S(1)}, u32[]{:S(2)}, u32[]{:S(2)}) %collective-permute-start.11) | collective-permute-done | bytes 98336 | tf_op jit(solution)/shard_map/ppermute | solution.py:22
  103.4 2.6 %collective-permute-done.12 = f32[3,32,1,256]{3,1,2,0:T(8,128)S(1)} collective-permute-done((f32[3,32,1,256]{3,1,2,0:T(8,128)S(1)}, f32[3,32,1,256]{3,1,2,0:T(8,128)S(1)}, u32[]{:S(2)}, u32[]{:S(2)}) %collective-permute-start.12) | collective-permute-done | bytes 98336 | tf_op jit(solution)/shard_map/ppermute | solution.py:23
  106.0 2.9 %collective-permute-done.13 = f32[3,32,1,256]{3,1,2,0:T(8,128)S(1)} collective-permute-done((f32[3,32,1,256]{3,1,2,0:T(8,128)S(1)}, f32[3,32,1,256]{3,1,2,0:T(8,128)S(1)}, u32[]{:S(2)}, u32[]{:S(2)}) %collective-permute-start.13) | collective-permute-done | bytes 98336 | tf_op jit(solution)/shard_map/ppermute | solution.py:22
  111.5 8.5 %all_to_all.62 = f32[4,4,128]{2,1,0:T(4,128)S(1)} all-to-all(f32[4,4,128]{2,1,0:T(4,128)S(1)} %bitcast.56), channel_id=1, replica_groups=mesh['grp'=2,'col'=4,'lev'=4] {'col'}, dimensions={0} | all-to-all | bytes 16384 | tf_op jit(solution)/shard_map/all_to_all | solution.py:90
  (84 shorter events, 27.9 us)
Async XLA Ops:
  2.0 30.2 %collective-permute-start = (f32[3,32,1,256]{3,1,2,0:T(8,128)S(1)}, f32[3,32,1,256]{3,1,2,0:T(8,128)S(1)}, u32[]{:S(2)}, u32[]{:S(2)}) collective-permute-start(f32[3,32,1,256]{3,1,2,0:T(8,128)S(1)} %get-tuple-element.22), channel_id=1, source_target_pairs={{4,0},{8,4},{12,8},{0,12},{5,1},{9,5},{13,9},{1,13},{6,2},{10,6},{... | collective-permute-start | bytes 294920 | tf_op jit(solution)/shard_map/ppermute | solution.py:23
  7.1 25.1 %collective-permute-start.1 = (f32[3,32,1,256]{3,1,2,0:T(8,128)S(1)}, f32[3,32,1,256]{3,1,2,0:T(8,128)S(1)}, u32[]{:S(2)}, u32[]{:S(2)}) collective-permute-start(f32[3,32,1,256]{3,1,2,0:T(8,128)S(1)} %get-tuple-element.23), channel_id=1, source_target_pairs={{0,4},{4,8},{8,12},{12,0},{1,5},{5,9},{9,13},{13,1},{2,6},{6,10},{... | collective-permute-start | bytes 294920 | tf_op jit(solution)/shard_map/ppermute | solution.py:22
  8.5 10.6 %all-to-all-start.1 = ((s32[4,4,1]{1,2,0:T(1,128)}), s32[4,4,1]{1,2,0:T(1,128)S(1)}, u32[]{:S(2)}, u32[]{:S(2)}) async-start(s32[4,4,1]{1,2,0:T(1,128)} %bitcast.4), calls=%async_computation.1 | async-start | bytes 4096 | tf_op jit(solution)/shard_map/all_to_all | solution.py:83
  19.1 8.7 %all-to-all-start = ((s32[4,4,1]{1,2,0:T(1,128)}), s32[4,4,1]{1,2,0:T(1,128)S(1)}, u32[]{:S(2)}, u32[]{:S(2)}) async-start(s32[4,4,1]{1,2,0:T(1,128)} %bitcast), calls=%async_computation | async-start | bytes 4096 | tf_op jit(solution)/shard_map/all_to_all | solution.py:82
  27.8 25.7 %all-to-all-start.2 = ((s32[4,4,128]{2,1,0:T(4,128)}), s32[4,4,128]{2,1,0:T(4,128)S(1)}, u32[]{:S(2)}, u32[]{:S(2)}) async-start(s32[4,4,128]{2,1,0:T(4,128)} %bitcast.6), calls=%async_computation.2 | async-start | bytes 16384 | tf_op jit(solution)/shard_map/all_to_all | solution.py:81
  32.8 6.1 %collective-permute-start.2 = (f32[3,32,1,256]{3,1,2,0:T(8,128)S(1)}, f32[3,32,1,256]{3,1,2,0:T(8,128)S(1)}, u32[]{:S(2)}, u32[]{:S(2)}) collective-permute-start(f32[3,32,1,256]{3,1,2,0:T(8,128)S(1)} %get-tuple-element.20), channel_id=1, source_target_pairs={{4,0},{8,4},{12,8},{0,12},{5,1},{9,5},{13,9},{1,13},{6,2},{10,6},{... | collective-permute-start | bytes 294920 | tf_op jit(solution)/shard_map/ppermute | solution.py:23
  36.7 6.5 %collective-permute-start.3 = (f32[3,32,1,256]{3,1,2,0:T(8,128)S(1)}, f32[3,32,1,256]{3,1,2,0:T(8,128)S(1)}, u32[]{:S(2)}, u32[]{:S(2)}) collective-permute-start(f32[3,32,1,256]{3,1,2,0:T(8,128)S(1)} %get-tuple-element.21), channel_id=1, source_target_pairs={{0,4},{4,8},{8,12},{12,0},{1,5},{5,9},{9,13},{13,1},{2,6},{6,10},{... | collective-permute-start | bytes 294920 | tf_op jit(solution)/shard_map/ppermute | solution.py:22
  43.7 5.6 %collective-permute-start.4 = (f32[3,32,1,256]{3,1,2,0:T(8,128)S(1)}, f32[3,32,1,256]{3,1,2,0:T(8,128)S(1)}, u32[]{:S(2)}, u32[]{:S(2)}) collective-permute-start(f32[3,32,1,256]{3,1,2,0:T(8,128)S(1)} %get-tuple-element.18), channel_id=1, source_target_pairs={{4,0},{8,4},{12,8},{0,12},{5,1},{9,5},{13,9},{1,13},{6,2},{10,6},{... | collective-permute-start | bytes 294920 | tf_op jit(solution)/shard_map/ppermute | solution.py:23
  43.8 7.0 %collective-permute-start.5 = (f32[3,32,1,256]{3,1,2,0:T(8,128)S(1)}, f32[3,32,1,256]{3,1,2,0:T(8,128)S(1)}, u32[]{:S(2)}, u32[]{:S(2)}) collective-permute-start(f32[3,32,1,256]{3,1,2,0:T(8,128)S(1)} %get-tuple-element.19), channel_id=1, source_target_pairs={{0,4},{4,8},{8,12},{12,0},{1,5},{5,9},{9,13},{13,1},{2,6},{6,10},{... | collective-permute-start | bytes 294920 | tf_op jit(solution)/shard_map/ppermute | solution.py:22
  51.3 7.3 %copy-start.4 = (bf16[2,32,8,256]{3,2,1,0:T(8,128)(2,1)S(1)}, bf16[2,32,8,256]{3,2,1,0:T(8,128)(2,1)}, u32[]{:S(2)}) copy-start(bf16[2,32,8,256]{3,2,1,0:T(8,128)(2,1)} %param.12) | copy-start | bytes 786436
  51.3 5.4 %collective-permute-start.6 = (f32[3,32,1,256]{3,1,2,0:T(8,128)S(1)}, f32[3,32,1,256]{3,1,2,0:T(8,128)S(1)}, u32[]{:S(2)}, u32[]{:S(2)}) collective-permute-start(f32[3,32,1,256]{3,1,2,0:T(8,128)S(1)} %get-tuple-element.16), channel_id=1, source_target_pairs={{4,0},{8,4},{12,8},{0,12},{5,1},{9,5},{13,9},{1,13},{6,2},{10,6},{... | collective-permute-start | bytes 294920 | tf_op jit(solution)/shard_map/ppermute | solution.py:23
  51.4 6.7 %collective-permute-start.7 = (f32[3,32,1,256]{3,1,2,0:T(8,128)S(1)}, f32[3,32,1,256]{3,1,2,0:T(8,128)S(1)}, u32[]{:S(2)}, u32[]{:S(2)}) collective-permute-start(f32[3,32,1,256]{3,1,2,0:T(8,128)S(1)} %get-tuple-element.17), channel_id=1, source_target_pairs={{0,4},{4,8},{8,12},{12,0},{1,5},{5,9},{9,13},{13,1},{2,6},{6,10},{... | collective-permute-start | bytes 294920 | tf_op jit(solution)/shard_map/ppermute | solution.py:22
  53.4 9.3 %all-to-all-start.4 = ((bf16[16,32,128]{2,1,0:T(8,128)(2,1)}), bf16[16,32,128]{2,1,0:T(8,128)(2,1)S(1)}, u32[]{:S(2)}, u32[]{:S(2)}) async-start(bf16[16,32,128]{2,1,0:T(8,128)(2,1)} %param.14), calls=%async_computation.4 | async-start | bytes 262144 | tf_op jit(solution)/shard_map/all_to_all | solution.py:78
  62.7 8.8 %all-to-all-start.3 = ((bf16[4,4,128]{2,1,0:T(4,128)(2,1)}), bf16[4,4,128]{2,1,0:T(4,128)(2,1)S(1)}, u32[]{:S(2)}, u32[]{:S(2)}) async-start(bf16[4,4,128]{2,1,0:T(4,128)(2,1)} %bitcast.8), calls=%async_computation.3 | async-start | bytes 8192 | tf_op jit(solution)/shard_map/all_to_all | solution.py:80
  71.5 9.0 %all-to-all-start.5 = ((bf16[4,4,128]{2,1,0:T(4,128)(2,1)}), bf16[4,4,128]{2,1,0:T(4,128)(2,1)S(1)}, u32[]{:S(2)}, u32[]{:S(2)}) async-start(bf16[4,4,128]{2,1,0:T(4,128)(2,1)} %bitcast.16), calls=%async_computation.5 | async-start | bytes 8192 | tf_op jit(solution)/shard_map/all_to_all | solution.py:79
  82.2 7.0 %collective-permute-start.8 = (f32[3,32,1,256]{3,1,2,0:T(8,128)S(1)}, f32[3,32,1,256]{3,1,2,0:T(8,128)S(1)}, u32[]{:S(2)}, u32[]{:S(2)}) collective-permute-start(f32[3,32,1,256]{3,1,2,0:T(8,128)S(1)} %get-tuple-element.14), channel_id=1, source_target_pairs={{4,0},{8,4},{12,8},{0,12},{5,1},{9,5},{13,9},{1,13},{6,2},{10,6},{... | collective-permute-start | bytes 294920 | tf_op jit(solution)/shard_map/ppermute | solution.py:23
  86.0 6.4 %collective-permute-start.9 = (f32[3,32,1,256]{3,1,2,0:T(8,128)S(1)}, f32[3,32,1,256]{3,1,2,0:T(8,128)S(1)}, u32[]{:S(2)}, u32[]{:S(2)}) collective-permute-start(f32[3,32,1,256]{3,1,2,0:T(8,128)S(1)} %get-tuple-element.15), channel_id=1, source_target_pairs={{0,4},{4,8},{8,12},{12,0},{1,5},{5,9},{9,13},{13,1},{2,6},{6,10},{... | collective-permute-start | bytes 294920 | tf_op jit(solution)/shard_map/ppermute | solution.py:22
  93.0 5.4 %collective-permute-start.10 = (f32[3,32,1,256]{3,1,2,0:T(8,128)S(1)}, f32[3,32,1,256]{3,1,2,0:T(8,128)S(1)}, u32[]{:S(2)}, u32[]{:S(2)}) collective-permute-start(f32[3,32,1,256]{3,1,2,0:T(8,128)S(1)} %get-tuple-element.12), channel_id=1, source_target_pairs={{4,0},{8,4},{12,8},{0,12},{5,1},{9,5},{13,9},{1,13},{6,2},{10,6},{... | collective-permute-start | bytes 294920 | tf_op jit(solution)/shard_map/ppermute | solution.py:23
  94.1 6.7 %collective-permute-start.11 = (f32[3,32,1,256]{3,1,2,0:T(8,128)S(1)}, f32[3,32,1,256]{3,1,2,0:T(8,128)S(1)}, u32[]{:S(2)}, u32[]{:S(2)}) collective-permute-start(f32[3,32,1,256]{3,1,2,0:T(8,128)S(1)} %get-tuple-element.13), channel_id=1, source_target_pairs={{0,4},{4,8},{8,12},{12,0},{1,5},{5,9},{9,13},{13,1},{2,6},{6,10},{... | collective-permute-start | bytes 294920 | tf_op jit(solution)/shard_map/ppermute | solution.py:22
  101.3 4.7 %collective-permute-start.12 = (f32[3,32,1,256]{3,1,2,0:T(8,128)S(1)}, f32[3,32,1,256]{3,1,2,0:T(8,128)S(1)}, u32[]{:S(2)}, u32[]{:S(2)}) collective-permute-start(f32[3,32,1,256]{3,1,2,0:T(8,128)S(1)} %get-tuple-element.10), channel_id=1, source_target_pairs={{4,0},{8,4},{12,8},{0,12},{5,1},{9,5},{13,9},{1,13},{6,2},{10,6},{... | collective-permute-start | bytes 294920 | tf_op jit(solution)/shard_map/ppermute | solution.py:23
  101.4 7.5 %collective-permute-start.13 = (f32[3,32,1,256]{3,1,2,0:T(8,128)S(1)}, f32[3,32,1,256]{3,1,2,0:T(8,128)S(1)}, u32[]{:S(2)}, u32[]{:S(2)}) collective-permute-start(f32[3,32,1,256]{3,1,2,0:T(8,128)S(1)} %get-tuple-element.11), channel_id=1, source_target_pairs={{0,4},{4,8},{8,12},{12,0},{1,5},{5,9},{9,13},{13,1},{2,6},{6,10},{... | collective-permute-start | bytes 294920 | tf_op jit(solution)/shard_map/ppermute | solution.py:22
  109.3 11.1 %copy-start.1 = (f32[2,32,8,256]{3,2,1,0:T(8,128)S(1)}, f32[2,32,8,256]{3,2,1,0:T(8,128)}, u32[]{:S(2)}) copy-start(f32[2,32,8,256]{3,2,1,0:T(8,128)} %param.11) | copy-start | bytes 1572868
  109.4 10.6 %collective-permute-start.14 = (f32[3,32,1,256]{3,1,2,0:T(8,128)S(1)}, f32[3,32,1,256]{3,1,2,0:T(8,128)S(1)}, u32[]{:S(2)}, u32[]{:S(2)}) collective-permute-start(f32[3,32,1,256]{3,1,2,0:T(8,128)S(1)} %get-tuple-element.8), channel_id=1, source_target_pairs={{4,0},{8,4},{12,8},{0,12},{5,1},{9,5},{13,9},{1,13},{6,2},{10,6},{... | collective-permute-start | bytes 294920 | tf_op jit(solution)/shard_map/ppermute | solution.py:23
  109.4 10.5 %collective-permute-start.15 = (f32[3,32,1,256]{3,1,2,0:T(8,128)S(1)}, f32[3,32,1,256]{3,1,2,0:T(8,128)S(1)}, u32[]{:S(2)}, u32[]{:S(2)}) collective-permute-start(f32[3,32,1,256]{3,1,2,0:T(8,128)S(1)} %get-tuple-element.9), channel_id=1, source_target_pairs={{0,4},{4,8},{8,12},{12,0},{1,5},{5,9},{9,13},{13,1},{2,6},{6,10},{... | collective-permute-start | bytes 294920 | tf_op jit(solution)/shard_map/ppermute | solution.py:22
  (4 other events, 16.2 us)
where the time goes:
time: 124 us; the launch traced here: 123 us
  waiting for transfers between devices  48.8 us (39%)
  starting transfers between devices  44.5 us (36%)
  blocking collectives  14.3 us (12%)
  local copies, waits for them, and re-layouts  7.28 us (6%)
  other arithmetic  7.09 us (6%)
    ppermute x8, waiting for transfers between devices, padded_2(): before = lax.ppermute(last, axis, up)  15.7 us
    ppermute x8, waiting for transfers between devices, padded_2(): after = lax.ppermute(initial, axis, down)  14.7 us
    ppermute x8, starting transfers between devices, padded_2(): after = lax.ppermute(initial, axis, down)  14.1 us
    ppermute x8, starting transfers between devices, padded_2(): before = lax.ppermute(last, axis, up)  9.06 us
    all_to_all x1, blocking collectives, local(): lax.all_to_all(departure, 'col', split_axis=0, concat_axis=0, tiled=True)  8.51 us
    psum x1, blocking collectives, solve_rows(): radiance = lax.psum(partial_value, 'lev')  5.77 us
    all_to_all x1, waiting for transfers between devices, local(): lax.all_to_all(obs_cell, 'col', split_axis=0, concat_axis=0, tiled=True)  5.42 us
    all_to_all x1, waiting for transfers between devices, local(): lax.all_to_all(obs_weight, 'col', split_axis=0, concat_axis=0, tiled=True)  5.39 us
  transfers between devices with their start and end apart: 22, of which 15 were waited for; matrix products, arithmetic and copies ran while one was open for 5% of the time, Pallas kernels for 0%

commit v1 on v0

--- a/solution.py
+++ b/solution.py
@@ -3,7 +3,11 @@
 import jax
 import jax.numpy as jnp
 from jax import lax
+from jax.experimental import pallas as pl
+from jax.experimental.pallas import tpu as pltpu
 from jax.sharding import PartitionSpec as P
+import functools
+import numpy as np
 
 STEPS = 4
 
@@ -97,6 +101,315 @@
     return (control + adjoint[0], control_ens + adjoint[1:], departures)
 
 
+LANES = 128
+
+
+def stencil_power():
+    step = np.array([[0.0, rate_x, 0.0], [rate_y, 1.0 - 2.0 * rate_x - 2.0 * rate_y, rate_y], [0.0, rate_x, 0.0]])
+    total = np.zeros((2 * STEPS + 1, 2 * STEPS + 1))
+    total[STEPS, STEPS] = 1.0
+    for _ in range(STEPS):
+        wide = np.pad(total, 1)
+        total = sum(
+            step[i, j] * wide[i : i + 2 * STEPS + 1, j : j + 2 * STEPS + 1]
+            for i in range(3)
+            for j in range(3)
+        )
+    return total[STEPS:, STEPS:]
+
+
+def split(value):
+    high = value.astype(jnp.bfloat16)
+    return high, (value - high.astype(jnp.float32)).astype(jnp.bfloat16)
+
+
+def dot(a, b, b_dim):
+    return lax.dot_general(a, b, (((1,), (b_dim,)), ((), ())), preferred_element_type=jnp.float32)
+
+
+def spread_groups(value, width):
+    total = value
+    for shift in range(width, LANES, width):
+        total = total + pltpu.roll(value, shift, 1)
+    return total
+
+
+def fused(
+    cfg,
+    ctl_hbm, cen_hbm, ens_hbm, spr_hbm, jac_hbm, val_ref, wgt_ref, msk_ref, cell_ref, count_ref,
+    octl_hbm, ocen_hbm, dep_ref,
+    ctl, cen, ens, ensf, spr, jac, cells, ey, fst, vst, wst, pv, pv_in, rad_in, a_all,
+    in_sem, out_sem, send_sem, recv_sem,
+):
+    cols, levs, slots, lev, cx, ny = cfg
+    cap = slots // cols
+    nx = cols * cx
+    every = cols * slots
+    me, my_lev = lax.axis_index("col"), lax.axis_index("lev")
+    table = stencil_power()
+
+    halves = range(ny // LANES)
+    lanes_of = [slice(h * LANES, (h + 1) * LANES) for h in halves]
+    pairs = [(ctl_hbm.at[:, lanes_of[h]], ctl.at[h]) for h in halves]
+    pairs += [(cen_hbm.at[e, :, lanes_of[h]], cen.at[e, h]) for e in range(2) for h in halves]
+    fields = len(pairs)
+    pairs += [(ens_hbm, ens)] + [(spr_hbm.at[:, lanes_of[h]], spr.at[h]) for h in halves]
+    pairs += [(jac_hbm, jac)]
+    loads = [pltpu.make_async_copy(src, dst, in_sem.at[i]) for i, (src, dst) in enumerate(pairs)]
+    for load in loads:
+        load.start()
+
+    barrier = pltpu.get_barrier_semaphore()
+    for d in range(1, cols):
+        pl.semaphore_signal(
+            barrier, inc=1, device_id={"col": lax.rem(me + d, cols)}, device_id_type=pl.DeviceIdType.MESH
+        )
+    for d in range(1, levs):
+        pl.semaphore_signal(
+            barrier, inc=1, device_id={"lev": lax.rem(my_lev + d, levs)}, device_id_type=pl.DeviceIdType.MESH
+        )
+
+    def send(phase, axis, peers, mine, src_of, dst):
+        copies = []
+        for d in range(1, peers):
+            to = lax.rem(mine + d, peers)
+            copy = pltpu.make_async_remote_copy(
+                src_ref=src_of(to),
+                dst_ref=dst,
+                send_sem=send_sem.at[phase, d],
+                recv_sem=recv_sem.at[phase, d],
+                device_id={axis: to},
+                device_id_type=pl.DeviceIdType.MESH,
+            )
+            copy.start()
+            copies.append(copy)
+        return copies
+
+    row = lax.broadcasted_iota(jnp.int32, (slots, LANES), 0)
+    lane = lax.broadcasted_iota(jnp.int32, (slots, LANES), 1)
+    own = jnp.zeros((slots, LANES), jnp.int32)
+    for r in range(slots):
+        own = jnp.where(row == r, cell_ref[r], own)
+    my_rows = pl.ds(pl.multiple_of(me * slots, slots), slots)
+    cells[my_rows, :] = own
+    pl.semaphore_wait(barrier, cols + levs - 2)
+    cell_copies = send(0, "col", cols, me, lambda to: cells.at[my_rows], cells.at[my_rows])
+
+    for load in loads[:fields]:
+        load.wait()
+    zeros = jnp.zeros((lev, ny), jnp.bfloat16)
+    picks = [pl.ds(x, lev, stride=cx) for x in range(cx)]
+    for x in range(cx):
+        for i, ref in enumerate((ctl, cen.at[0], cen.at[1])):
+            for h in halves:
+                high, low = split(ref.at[h][picks[x], :])
+                fst[x, i * lev : (i + 1) * lev, lanes_of[h]] = high
+                fst[x, LANES + i * lev : LANES + (i + 1) * lev, lanes_of[h]] = low
+        fst[x, 3 * lev : 4 * lev, :] = zeros
+        fst[x, LANES + 3 * lev : LANES + 4 * lev, :] = zeros
+    for load in loads[fields:-1]:
+        load.wait()
+    for e in range(2):
+        member = ens[e].astype(jnp.float32).reshape(lev * cx, ny)
+        for h in halves:
+            ensf[e, h] = member[:, lanes_of[h]]
+    for x in range(cx):
+        for h in halves:
+            high, low = split(spr.at[h][picks[x], :])
+            vst[x, 0:lev, lanes_of[h]] = high
+            vst[x, lev : 2 * lev, lanes_of[h]] = ensf.at[0, h][picks[x], :].astype(jnp.bfloat16)
+            vst[x, 2 * lev : 3 * lev, lanes_of[h]] = ensf.at[1, h][picks[x], :].astype(jnp.bfloat16)
+            vst[x, 3 * lev : 4 * lev, lanes_of[h]] = low
+
+    for copy in cell_copies:
+        copy.wait()
+
+    cell = cells[...]
+    shift = ny.bit_length() - 1
+    cell_x = lax.shift_right_logical(cell, jnp.full_like(cell, shift))
+    cell_y = cell & (ny - 1)
+    slot = lax.broadcasted_iota(jnp.int32, (every, LANES), 0)
+    target = lax.shift_right_logical(slot, jnp.full_like(slot, cap.bit_length() - 1)) & (cols - 1)
+    apart = me * cx - (target * cx + cell_x)
+    y_lane = lax.broadcasted_iota(jnp.int32, (every, LANES), 1)
+    for h in range(ny // LANES):
+        y = y_lane + h * LANES
+        dy = jnp.abs(y - cell_y)
+        below = y + cell_y + 2
+        above = 2 * ny - y - cell_y
+        for m in range(STEPS + 1):
+            one = jnp.where(dy == m, 1.0, 0.0)
+            if m >= 2:
+                one = one - jnp.where((below == m) | (above == m), 1.0, 0.0)
+            ey[m, :, h * LANES : (h + 1) * LANES] = one
+    out = None
+    for x in range(cx):
+        dx = apart + x
+        dx = jnp.where(dx >= nx // 2, dx - nx, dx)
+        dx = jnp.abs(jnp.where(dx < -(nx // 2), dx + nx, dx))
+        at = [dx == q for q in range(STEPS + 1)]
+        factors = []
+        for m in range(STEPS + 1):
+            factor = jnp.zeros((every, LANES), jnp.float32)
+            for q in range(STEPS + 1 - m):
+                factor = jnp.where(at[q], float(table[q, m]), factor)
+            factors.append(factor)
+        here = jnp.where(at[0], 1.0, 0.0)
+        hits = []
+        for h in range(ny // LANES):
+            part = slice(h * LANES, (h + 1) * LANES)
+            centre = ey[0, :, part]
+            weight = factors[0] * centre
+            for m in range(1, STEPS + 1):
+                weight = weight + factors[m] * ey[m, :, part]
+            high, low = split(weight)
+            wst[x, 0:every, part] = high
+            wst[x, every : 2 * every, part] = low
+            wst[x, 2 * every : 3 * every, part] = high
+            hits.append((here * centre).astype(jnp.bfloat16))
+        sums = dot(wst[x, 0 : 2 * every, :], fst[x], 1)
+        found = dot(jnp.concatenate(hits, axis=1), vst[x], 1)
+        out = (sums, found) if out is None else (out[0] + sums, out[1] + found)
+    sums, found = out
+    pv[:, 0:LANES] = sums[0:every, 0:LANES] + sums[0:every, LANES:] + sums[every:, 0:LANES]
+    group = lax.shift_right_logical(y_lane, jnp.full_like(y_lane, lev.bit_length() - 1))
+    found = jnp.where(group == 0, found + pltpu.roll(found, lev, 1), found * (1.0 / math.sqrt(2)))
+    pv[:, LANES:] = jnp.where(group == 3, 0.0, found)
+    pv_in[me] = pv[my_rows, :]
+    copies = send(
+        1, "col", cols, me,
+        lambda to: pv.at[pl.ds(pl.multiple_of(to * slots, slots), slots)], pv_in.at[me],
+    )
+    loads[-1].wait()
+    for copy in copies:
+        copy.wait()
+
+    both = pv_in[0]
+    for s in range(1, cols):
+        both = both + pv_in[s]
+    values = both[:, LANES:]
+    columns = spread_groups(both[:, 0:LANES] * values, lev)
+    jac_rows = jac[...].reshape(slots * lev, LANES)
+    per = LANES // lev
+    lane_group = lax.shift_right_logical(lane, jnp.full_like(lane, lev.bit_length() - 1))
+    tiles = slots // per
+    block = jnp.concatenate(
+        [jnp.where(row == q * per + lane_group, columns, 0.0) for q in range(tiles)], axis=1
+    ).astype(jnp.bfloat16)
+    rad_in[my_lev] = dot(block, jac_rows, 0)
+    for copy in send(2, "lev", levs, my_lev, lambda to: rad_in.at[my_lev], rad_in.at[my_lev]):
+        copy.wait()
+    radiance = rad_in[0]
+    for s in range(1, levs):
+        radiance = radiance + rad_in[s]
+
+    filled = jnp.zeros((slots, LANES), jnp.bool_)
+    for t in range(cols):
+        filled = filled | ((row >= t * cap) & (row < t * cap + jnp.minimum(count_ref[0, t], cap)))
+    departure = jnp.where(
+        filled & (msk_ref[...] > 0),
+        wgt_ref[...].astype(jnp.float32) * (radiance - val_ref[...].astype(jnp.float32)),
+        0.0,
+    )
+    dep_ref[...] = departure
+    spread_out = dot(departure.astype(jnp.bfloat16), jac_rows, 1)
+    increment = jnp.zeros((slots, LANES), jnp.float32)
+    for q in range(tiles):
+        part = spread_out[:, q * LANES : (q + 1) * LANES]
+        increment = increment + jnp.where(row == q * per + lane_group, part, 0.0)
+    increment = spread_groups(increment, lev)
+    a_all[my_rows, :] = increment * values
+    for copy in send(3, "col", cols, me, lambda to: a_all.at[my_rows], a_all.at[my_rows]):
+        copy.wait()
+
+    amount = a_all[...]
+    a_high, a_low = split(amount)
+    a_high, a_low = a_high.astype(jnp.float32), a_low.astype(jnp.float32)
+    left = jnp.concatenate([a_high, a_high, a_low, jnp.zeros_like(a_low)], axis=0).T
+    left = left[:, 0 : 3 * every].astype(jnp.bfloat16)
+    for x in range(cx):
+        add = dot(left, wst[x], 0)
+        for i, ref in enumerate((ctl, cen.at[0], cen.at[1])):
+            for h in halves:
+                here = ref.at[h]
+                here[picks[x], :] = here[picks[x], :] + add[i * lev : (i + 1) * lev, lanes_of[h]]
+    pairs = [(ctl.at[h], octl_hbm.at[:, lanes_of[h]]) for h in halves]
+    pairs += [(cen.at[e, h], ocen_hbm.at[e, :, lanes_of[h]]) for e in range(2) for h in halves]
+    stores = [pltpu.make_async_copy(src, dst, out_sem.at[i]) for i, (src, dst) in enumerate(pairs)]
+    for store in stores:
+        store.start()
+    for store in stores:
+        store.wait()
+
+
+def fits(members, levels, cells_x, cells_y, slot_total, channels, peers):
+    def power(n):
+        return n & (n - 1) == 0
+    return (
+        members == 2 and levels * 4 == LANES and channels == LANES and cells_x == 8
+        and cells_y % LANES == 0 and power(cells_y) and cells_y <= 256 and power(peers) and slot_total % 16 == 0
+        and power(slot_total // peers) and peers * slot_total * 3 <= 256
+        and peers * cells_x > 2 * STEPS
+    )
+
+
+def local_fused(control, control_ens, ensemble, spread, jacobian, obs_value, obs_weight, channel_mask, obs_cell, obs_count):
+    members = control_ens.shape[0]
+    levels, cells_x, cells_y = control.shape
+    slots, _, channels = jacobian.shape
+    cols, levs = lax.axis_size("col"), lax.axis_size("lev")
+    every = cols * slots
+    flat = (levels * cells_x, cells_y)
+    cut = (cells_y // LANES, levels * cells_x, LANES)
+    any_space = pl.BlockSpec(memory_space=pl.ANY)
+    vmem = pl.BlockSpec(memory_space=pltpu.VMEM)
+    smem = pl.BlockSpec(memory_space=pltpu.SMEM)
+    out_control, out_ens, departures = pl.pallas_call(
+        functools.partial(fused, (cols, levs, slots, levels, cells_x, cells_y)),
+        out_shape=(
+            jax.ShapeDtypeStruct(flat, jnp.float32),
+            jax.ShapeDtypeStruct((members,) + flat, jnp.float32),
+            jax.ShapeDtypeStruct((slots, channels), jnp.float32),
+        ),
+        in_specs=[any_space] * 5 + [vmem] * 3 + [smem] * 2,
+        out_specs=(any_space, any_space, vmem),
+        scratch_shapes=[
+            pltpu.VMEM(cut, jnp.float32),
+            pltpu.VMEM((members,) + cut, jnp.float32),
+            pltpu.VMEM(ensemble.shape, jnp.bfloat16),
+            pltpu.VMEM((members,) + cut, jnp.float32),
+            pltpu.VMEM(cut, jnp.float32),
+            pltpu.VMEM(jacobian.shape, jnp.bfloat16),
+            pltpu.VMEM((every, LANES), jnp.int32),
+            pltpu.VMEM((STEPS + 1, every, cells_y), jnp.float32),
+            pltpu.VMEM((cells_x, 2 * LANES, cells_y), jnp.bfloat16),
+            pltpu.VMEM((cells_x, LANES, cells_y), jnp.bfloat16),
+            pltpu.VMEM((cells_x, 3 * every, cells_y), jnp.bfloat16),
+            pltpu.VMEM((every, 2 * LANES), jnp.float32),
+            pltpu.VMEM((cols, slots, 2 * LANES), jnp.float32),
+            pltpu.VMEM((levs, slots, LANES), jnp.float32),
+            pltpu.VMEM((every, LANES), jnp.float32),
+            pltpu.SemaphoreType.DMA((2 + (members + 2) * cut[0],)),
+            pltpu.SemaphoreType.DMA(((members + 1) * cut[0],)),
+            pltpu.SemaphoreType.DMA((4, max(cols, levs))),
+            pltpu.SemaphoreType.DMA((4, max(cols, levs))),
+        ],
+        compiler_params=pltpu.CompilerParams(
+            collective_id=0, has_side_effects=True, vmem_limit_bytes=32 * 1024 * 1024
+        ),
+    )(
+        control.reshape(flat), control_ens.reshape((members,) + flat), ensemble, spread.reshape(flat),
+        jacobian, obs_value, obs_weight, channel_mask, obs_cell, obs_count,
+    )
+    return out_control.reshape(control.shape), out_ens.reshape(control_ens.shape), departures
+
+
+def pick_local(control, control_ens, ensemble, spread, jacobian, *obs):
+    sizes = (control_ens.shape[0],) + control.shape + (jacobian.shape[0], jacobian.shape[2], lax.axis_size("col"))
+    run = local_fused if fits(*sizes) else local
+    return run(control, control_ens, ensemble, spread, jacobian, *obs)
+
+
 def solution(mesh):
     placed = (
         P(("grp", "lev"), "col", None),
@@ -111,7 +424,7 @@
         P(("grp", "col"), None),
     )
     return jax.shard_map(
-        local,
+        pick_local,
         mesh=mesh,
         in_specs=placed,
         out_specs=(

time: 124 us -> 31.5 us (0.25)
  waiting for transfers between devices: 48.8 us -> 0 us
  starting transfers between devices: 44.5 us -> 0 us
  Pallas kernels: 0 us -> 21.5 us
  blocking collectives: 14.3 us -> 0 us
  other arithmetic: 7.09 us -> 0 us
  local copies, waits for them, and re-layouts: 7.28 us -> 8.94 us
    ppermute x16 -> x0, waiting for transfers between devices: 30.3 us -> none  [the longest x8 15.7 us: padded_2(): before = lax.ppermute(last, axis, up)]
    ppermute x16 -> x0, starting transfers between devices: 23.1 us -> none  [the longest x8 14.1 us: padded_2(): after = lax.ppermute(initial, axis, down)]
    pallas_call x0 -> x1, Pallas kernels: none -> 21.5 us  [local_fused(): pl.pallas_call(functools.partial(fused, (cols, levs, slots, levels, cells...]
    all_to_all x6 -> x0, starting transfers between devices: 21.4 us -> none  [the longest x1 5.08 us: local(): lax.all_to_all(filled, 'col', split_axis=0, concat_axis=0, tiled=True)]
    all_to_all x6 -> x0, waiting for transfers between devices: 18.5 us -> none  [the longest x1 5.42 us: local(): lax.all_to_all(obs_cell, 'col', split_axis=0, concat_axis=0, tiled=True)]
    all_to_all x1 -> x0, blocking collectives: 8.51 us -> none  [local(): lax.all_to_all(departure, 'col', split_axis=0, concat_axis=0, tiled=True)]
    psum x1 -> x0, blocking collectives: 5.77 us -> none  [solve_rows(): radiance = lax.psum(partial_value, 'lev')]
    unnamed x17 -> x23, local copies, waits for them, and re-layouts: 3.93 us -> 8.94 us
  transfers between devices with their start and end apart: 22 -> 0, of which waited for: 15 -> 0; matrix products, arithmetic and copies ran while one was open for 5% -> 0% of each run, Pallas kernels for 0% -> 0%
where the time goes in v1:
time: 31.5 us; the launch traced here: 31.1 us
  Pallas kernels  21.5 us (68%)
  local copies, waits for them, and re-layouts  8.94 us (28%)
  between operations  0.68 us (2%)
    pallas_call x1, Pallas kernels, local_fused(): pl.pallas_call(functools.partial(fused, (cols, levs, slots, levels, cells...  21.5 us
    unnamed x23, local copies, waits for them, and re-layouts  8.94 us

profile of v1, /device:TPU:0, one launch (start us, length us, event | category | flops | bytes accessed | tf_op | source)
XLA Modules:
  0.0 31.1 jit_solution(7612333360199789198)
XLA Ops:
  0.6 0.0 copy-start.6
  0.6 0.0 copy-start.8
  0.7 0.0 copy-start.9
  0.7 0.7 %copy-done.6 = bf16[16,128]{1,0:T(8,128)(2,1)S(1)} copy-done((bf16[16,128]{1,0:T(8,128)(2,1)S(1)}, bf16[16,128]{1,0:T(8,128)(2,1)}, u32[]{:S(2)}) %copy-start.6) | copy-done | bytes 4120
  1.3 0.0 copy-done.8
  1.3 0.0 copy-done.9
  1.3 0.0 copy-start
  1.3 1.0 %copy-done = f32[2,32,8,256]{3,2,1,0:T(8,128)S(1)} copy-done((f32[2,32,8,256]{3,2,1,0:T(8,128)S(1)}, f32[2,32,8,256]{3,2,1,0:T(8,128)}, u32[]{:S(2)}) %copy-start) | copy-done | bytes 524312
  2.4 0.0 copy-start.1
  2.4 0.9 %copy-done.1 = f32[32,8,256]{2,1,0:T(8,128)S(1)} copy-done((f32[32,8,256]{2,1,0:T(8,128)S(1)}, f32[32,8,256]{2,1,0:T(8,128)}, u32[]{:S(2)}) %copy-start.1) | copy-done | bytes 262168
  3.3 0.0 copy-start.2
  3.3 0.9 %copy-done.2 = bf16[2,32,8,256]{3,2,1,0:T(8,128)(2,1)S(1)} copy-done((bf16[2,32,8,256]{3,2,1,0:T(8,128)(2,1)S(1)}, bf16[2,32,8,256]{3,2,1,0:T(8,128)(2,1)}, u32[]{:S(2)}) %copy-start.2) | copy-done | bytes 262168
  4.3 0.0 copy-start.3
  4.3 0.9 %copy-done.3 = f32[32,8,256]{2,1,0:T(8,128)S(1)} copy-done((f32[32,8,256]{2,1,0:T(8,128)S(1)}, f32[32,8,256]{2,1,0:T(8,128)}, u32[]{:S(2)}) %copy-start.3) | copy-done | bytes 262168
  5.2 0.0 copy-start.4
  5.2 0.9 %copy-done.4 = bf16[16,32,128]{2,1,0:T(8,128)(2,1)S(1)} copy-done((bf16[16,32,128]{2,1,0:T(8,128)(2,1)S(1)}, bf16[16,32,128]{2,1,0:T(8,128)(2,1)}, u32[]{:S(2)}) %copy-start.4) | copy-done | bytes 131096
  6.1 0.0 copy-start.5
  6.1 0.7 %copy-done.5 = s32[16,128]{1,0:T(8,128)S(1)} copy-done((s32[16,128]{1,0:T(8,128)S(1)}, s32[16,128]{1,0:T(8,128)}, u32[]{:S(2)}) %copy-start.5) | copy-done | bytes 8216
  6.8 0.0 copy-start.7
  6.8 0.7 %copy-done.7 = bf16[16,128]{1,0:T(8,128)(2,1)S(1)} copy-done((bf16[16,128]{1,0:T(8,128)(2,1)S(1)}, bf16[16,128]{1,0:T(8,128)(2,1)}, u32[]{:S(2)}) %copy-start.7) | copy-done | bytes 4120
  7.5 21.5 %shard_map.121 = (f32[256,256]{1,0:T(8,128)S(1)}, f32[2,256,256]{2,1,0:T(8,128)S(1)}, f32[16,128]{1,0:T(8,128)S(1)}) custom-call(f32[256,256]{1,0:T(8,128)S(1)} %bitcast.7, f32[2,256,256]{2,1,0:T(8,128)S(1)} %bitcast.5, bf16[2,32,8,256]{3,2,1,0:T(8,128)(2,1)S(1)} %copy-done.2, f32[256,256]{1,0:T(8,128)S(1)} %bitcast.8, bf16[16,32,128]{2,1,0:T(8,128)(2,1)S(1)} %copy-done.4, ...), custom_call_target="tpu_custom_call" | custom-call | tf_op jit(solution)/shard_map/pallas_call | solution.py:367
  29.0 0.7 %copy.16 = f32[32,8,256]{2,1,0:T(8,128)} copy(f32[32,8,256]{2,1,0:T(8,128)S(1)} %bitcast.9) | data formatting | bytes 524288
  29.7 0.8 %copy.17 = f32[2,32,8,256]{3,2,1,0:T(8,128)} copy(f32[2,32,8,256]{3,2,1,0:T(8,128)S(1)} %bitcast.6) | data formatting | bytes 1048576
  30.5 0.6 %copy.18 = f32[16,128]{1,0:T(8,128)} copy(f32[16,128]{1,0:T(8,128)S(1)} %get-tuple-element.14) | data formatting | bytes 16384
Async XLA Ops:
  0.6 0.7 %copy-start.6 = (bf16[16,128]{1,0:T(8,128)(2,1)S(1)}, bf16[16,128]{1,0:T(8,128)(2,1)}, u32[]{:S(2)}) copy-start(bf16[16,128]{1,0:T(8,128)(2,1)} %val_ref.1) | copy-start | bytes 12292
  0.6 0.7 %copy-start.8 = (s32[16]{0:T(128)S(1)}, s32[16]{0:T(128)}, u32[]{:S(2)}) copy-start(s32[16]{0:T(128)} %cell_ref.1) | copy-start | bytes 196
  0.7 0.7 %copy-start.9 = (s32[1,4]{1,0:T(1,128)S(1)}, s32[1,4]{1,0:T(1,128)}, u32[]{:S(2)}) copy-start(s32[1,4]{1,0:T(1,128)} %count_ref.1) | copy-start | bytes 52
  1.3 1.0 %copy-start = (f32[2,32,8,256]{3,2,1,0:T(8,128)S(1)}, f32[2,32,8,256]{3,2,1,0:T(8,128)}, u32[]{:S(2)}) copy-start(f32[2,32,8,256]{3,2,1,0:T(8,128)} %param.11) | copy-start | bytes 1572868
  2.4 0.9 %copy-start.1 = (f32[32,8,256]{2,1,0:T(8,128)S(1)}, f32[32,8,256]{2,1,0:T(8,128)}, u32[]{:S(2)}) copy-start(f32[32,8,256]{2,1,0:T(8,128)} %param.10) | copy-start | bytes 786436
  3.3 0.9 %copy-start.2 = (bf16[2,32,8,256]{3,2,1,0:T(8,128)(2,1)S(1)}, bf16[2,32,8,256]{3,2,1,0:T(8,128)(2,1)}, u32[]{:S(2)}) copy-start(bf16[2,32,8,256]{3,2,1,0:T(8,128)(2,1)} %ens_hbm.1) | copy-start | bytes 786436
  4.3 0.9 %copy-start.3 = (f32[32,8,256]{2,1,0:T(8,128)S(1)}, f32[32,8,256]{2,1,0:T(8,128)}, u32[]{:S(2)}) copy-start(f32[32,8,256]{2,1,0:T(8,128)} %param.13) | copy-start | bytes 786436
  5.2 0.9 %copy-start.4 = (bf16[16,32,128]{2,1,0:T(8,128)(2,1)S(1)}, bf16[16,32,128]{2,1,0:T(8,128)(2,1)}, u32[]{:S(2)}) copy-start(bf16[16,32,128]{2,1,0:T(8,128)(2,1)} %jac_hbm.1) | copy-start | bytes 393220
  6.1 0.7 %copy-start.5 = (s32[16,128]{1,0:T(8,128)S(1)}, s32[16,128]{1,0:T(8,128)}, u32[]{:S(2)}) copy-start(s32[16,128]{1,0:T(8,128)} %msk_ref.1) | copy-start | bytes 24580
  6.8 0.7 %copy-start.7 = (bf16[16,128]{1,0:T(8,128)(2,1)S(1)}, bf16[16,128]{1,0:T(8,128)(2,1)}, u32[]{:S(2)}) copy-start(bf16[16,128]{1,0:T(8,128)(2,1)} %wgt_ref.1) | copy-start | bytes 12292

commit v2 on v1

--- a/solution.py
+++ b/solution.py
@@ -136,9 +136,9 @@
 
 def fused(
     cfg,
-    ctl_hbm, cen_hbm, ens_hbm, spr_hbm, jac_hbm, val_ref, wgt_ref, msk_ref, cell_ref, count_ref,
-    octl_hbm, ocen_hbm, dep_ref,
-    ctl, cen, ens, ensf, spr, jac, cells, ey, fst, vst, wst, pv, pv_in, rad_in, a_all,
+    ctl_hbm, cen_hbm, ens_hbm, spr_hbm, jac_hbm, val_hbm, wgt_hbm, msk_hbm, cell_hbm, count_hbm,
+    wst_hbm, a_hbm, dep_hbm,
+    ctl, cen, ens, ensf, spr, jac, val_ref, wgt_ref, msk_ref, cell_ref, count_ref, cells, dep_ref, ey, fst, vst, wst, found_ref, pv, pv_in, rad_in, a_all,
     in_sem, out_sem, send_sem, recv_sem,
 ):
     cols, levs, slots, lev, cx, ny = cfg
@@ -147,6 +147,7 @@
     every = cols * slots
     me, my_lev = lax.axis_index("col"), lax.axis_index("lev")
     table = stencil_power()
+    parts = slots // max(8, cap)
 
     halves = range(ny // LANES)
     lanes_of = [slice(h * LANES, (h + 1) * LANES) for h in halves]
@@ -154,11 +155,11 @@
     pairs += [(cen_hbm.at[e, :, lanes_of[h]], cen.at[e, h]) for e in range(2) for h in halves]
     fields = len(pairs)
     pairs += [(ens_hbm, ens)] + [(spr_hbm.at[:, lanes_of[h]], spr.at[h]) for h in halves]
-    pairs += [(jac_hbm, jac)]
+    small = len(pairs)
+    pairs += [(jac_hbm, jac), (val_hbm, val_ref), (wgt_hbm, wgt_ref), (msk_hbm, msk_ref), (count_hbm, count_ref)]
+    pairs += [(cell_hbm, cell_ref)]
     loads = [pltpu.make_async_copy(src, dst, in_sem.at[i]) for i, (src, dst) in enumerate(pairs)]
-    for load in loads:
-        load.start()
-
+    loads[-1].start()
     barrier = pltpu.get_barrier_semaphore()
     for d in range(1, cols):
         pl.semaphore_signal(
@@ -168,6 +169,9 @@
         pl.semaphore_signal(
             barrier, inc=1, device_id={"lev": lax.rem(my_lev + d, levs)}, device_id_type=pl.DeviceIdType.MESH
         )
+
+    for load in loads[:-1]:
+        load.start()
 
     def send(phase, axis, peers, mine, src_of, dst):
         copies = []
@@ -185,6 +189,7 @@
             copies.append(copy)
         return copies
 
+    loads[-1].wait()
     row = lax.broadcasted_iota(jnp.int32, (slots, LANES), 0)
     lane = lax.broadcasted_iota(jnp.int32, (slots, LANES), 1)
     own = jnp.zeros((slots, LANES), jnp.int32)
@@ -207,7 +212,7 @@
                 fst[x, LANES + i * lev : LANES + (i + 1) * lev, lanes_of[h]] = low
         fst[x, 3 * lev : 4 * lev, :] = zeros
         fst[x, LANES + 3 * lev : LANES + 4 * lev, :] = zeros
-    for load in loads[fields:-1]:
+    for load in loads[fields:small]:
         load.wait()
     for e in range(2):
         member = ens[e].astype(jnp.float32).reshape(lev * cx, ny)
@@ -271,24 +276,36 @@
         found = dot(jnp.concatenate(hits, axis=1), vst[x], 1)
         out = (sums, found) if out is None else (out[0] + sums, out[1] + found)
     sums, found = out
-    pv[:, 0:LANES] = sums[0:every, 0:LANES] + sums[0:every, LANES:] + sums[every:, 0:LANES]
+    wst_store = pltpu.make_async_copy(wst, wst_hbm, out_sem.at[0])
+    wst_store.start()
+    sums = sums[0:every, 0:LANES] + sums[0:every, LANES:] + sums[every:, 0:LANES]
     group = lax.shift_right_logical(y_lane, jnp.full_like(y_lane, lev.bit_length() - 1))
     found = jnp.where(group == 0, found + pltpu.roll(found, lev, 1), found * (1.0 / math.sqrt(2)))
-    pv[:, LANES:] = jnp.where(group == 3, 0.0, found)
-    pv_in[me] = pv[my_rows, :]
-    copies = send(
-        1, "col", cols, me,
-        lambda to: pv.at[pl.ds(pl.multiple_of(to * slots, slots), slots)], pv_in.at[me],
-    )
-    loads[-1].wait()
+    found_ref[...] = jnp.where(group == 3, 0.0, found)
+    window = slots // parts
+    for s in range(cols):
+        pv[s, 0:slots, :] = sums[s * slots : (s + 1) * slots]
+        start = s * slots + lax.div(me * cap, window) * window
+        pv[s, slots:, :] = found_ref[pl.ds(pl.multiple_of(start, window), window), :]
+    pv_in[me] = pv[me]
+    copies = send(1, "col", cols, me, lambda to: pv.at[to], pv_in.at[me])
+    for load in loads[small:-1]:
+        load.wait()
     for copy in copies:
         copy.wait()
 
-    both = pv_in[0]
+    fields_at = pv_in[0, 0:slots, :]
     for s in range(1, cols):
-        both = both + pv_in[s]
-    values = both[:, LANES:]
-    columns = spread_groups(both[:, 0:LANES] * values, lev)
+        fields_at = fields_at + pv_in[s, 0:slots, :]
+    per_part = cols // parts
+    pieces = []
+    for p in range(parts):
+        piece = pv_in[p * per_part, slots:, :]
+        for s in range(p * per_part + 1, (p + 1) * per_part):
+            piece = piece + pv_in[s, slots:, :]
+        pieces.append(piece)
+    values = jnp.concatenate(pieces, axis=0) if parts > 1 else pieces[0]
+    columns = spread_groups(fields_at * values, lev)
     jac_rows = jac[...].reshape(slots * lev, LANES)
     per = LANES // lev
     lane_group = lax.shift_right_logical(lane, jnp.full_like(lane, lev.bit_length() - 1))
@@ -312,6 +329,8 @@
         0.0,
     )
     dep_ref[...] = departure
+    dep_store = pltpu.make_async_copy(dep_ref, dep_hbm, out_sem.at[out_sem.shape[0] - 1])
+    dep_store.start()
     spread_out = dot(departure.astype(jnp.bfloat16), jac_rows, 1)
     increment = jnp.zeros((slots, LANES), jnp.float32)
     for q in range(tiles):
@@ -322,22 +341,51 @@
     for copy in send(3, "col", cols, me, lambda to: a_all.at[my_rows], a_all.at[my_rows]):
         copy.wait()
 
-    amount = a_all[...]
-    a_high, a_low = split(amount)
+    a_store = pltpu.make_async_copy(a_all, a_hbm, out_sem.at[1])
+    a_store.start()
+    for store in (wst_store, a_store, dep_store):
+        store.wait()
+
+
+def adjoint(
+    cfg, ctl_hbm, cen_hbm, wst_hbm, a_hbm, dep_hbm, octl_hbm, ocen_hbm, odep_hbm,
+    ctl, cen, wst, amount, dep, in_sem, out_sem,
+):
+    lev, cx, ny = cfg
+    halves = range(ny // LANES)
+    lanes_of = [slice(h * LANES, (h + 1) * LANES) for h in halves]
+    pairs = [(a_hbm, amount), (wst_hbm, wst)]
+    for h in halves:
+        pairs += [(ctl_hbm.at[:, lanes_of[h]], ctl.at[h])]
+        pairs += [(cen_hbm.at[e, :, lanes_of[h]], cen.at[e, h]) for e in range(2)]
+    pairs += [(dep_hbm, dep)]
+    loads = [pltpu.make_async_copy(src, dst, in_sem.at[i]) for i, (src, dst) in enumerate(pairs)]
+    for load in loads:
+        load.start()
+    loads[0].wait()
+    every = amount.shape[0]
+    a_high, a_low = split(amount[...])
     a_high, a_low = a_high.astype(jnp.float32), a_low.astype(jnp.float32)
     left = jnp.concatenate([a_high, a_high, a_low, jnp.zeros_like(a_low)], axis=0).T
     left = left[:, 0 : 3 * every].astype(jnp.bfloat16)
-    for x in range(cx):
-        add = dot(left, wst[x], 0)
-        for i, ref in enumerate((ctl, cen.at[0], cen.at[1])):
-            for h in halves:
-                here = ref.at[h]
-                here[picks[x], :] = here[picks[x], :] + add[i * lev : (i + 1) * lev, lanes_of[h]]
-    pairs = [(ctl.at[h], octl_hbm.at[:, lanes_of[h]]) for h in halves]
-    pairs += [(cen.at[e, h], ocen_hbm.at[e, :, lanes_of[h]]) for e in range(2) for h in halves]
-    stores = [pltpu.make_async_copy(src, dst, out_sem.at[i]) for i, (src, dst) in enumerate(pairs)]
-    for store in stores:
-        store.start()
+    loads[1].wait()
+    stores = []
+    for h in halves:
+        for load in loads[2 + 3 * h : 5 + 3 * h]:
+            load.wait()
+        for x in range(cx):
+            pick = pl.ds(x, lev, stride=cx)
+            add = dot(left, wst[x, :, lanes_of[h]], 0)
+            for i, ref in enumerate((ctl.at[h], cen.at[0, h], cen.at[1, h])):
+                ref[pick, :] = ref[pick, :] + add[i * lev : (i + 1) * lev]
+        pairs = [(ctl.at[h], octl_hbm.at[:, lanes_of[h]])]
+        pairs += [(cen.at[e, h], ocen_hbm.at[e, :, lanes_of[h]]) for e in range(2)]
+        for src, dst in pairs:
+            stores.append(pltpu.make_async_copy(src, dst, out_sem.at[len(stores)]))
+            stores[-1].start()
+    loads[-1].wait()
+    stores.append(pltpu.make_async_copy(dep, odep_hbm, out_sem.at[len(stores)]))
+    stores[-1].start()
     for store in stores:
         store.wait()
 
@@ -361,18 +409,16 @@
     every = cols * slots
     flat = (levels * cells_x, cells_y)
     cut = (cells_y // LANES, levels * cells_x, LANES)
-    any_space = pl.BlockSpec(memory_space=pl.ANY)
-    vmem = pl.BlockSpec(memory_space=pltpu.VMEM)
-    smem = pl.BlockSpec(memory_space=pltpu.SMEM)
-    out_control, out_ens, departures = pl.pallas_call(
+    hbm = pl.BlockSpec(memory_space=pltpu.HBM)
+    weights, amount, held = pl.pallas_call(
         functools.partial(fused, (cols, levs, slots, levels, cells_x, cells_y)),
         out_shape=(
-            jax.ShapeDtypeStruct(flat, jnp.float32),
-            jax.ShapeDtypeStruct((members,) + flat, jnp.float32),
+            jax.ShapeDtypeStruct((cells_x, 3 * every, cells_y), jnp.bfloat16),
+            jax.ShapeDtypeStruct((every, LANES), jnp.float32),
             jax.ShapeDtypeStruct((slots, channels), jnp.float32),
         ),
-        in_specs=[any_space] * 5 + [vmem] * 3 + [smem] * 2,
-        out_specs=(any_space, any_space, vmem),
+        in_specs=[hbm] * 10,
+        out_specs=(hbm, hbm, hbm),
         scratch_shapes=[
             pltpu.VMEM(cut, jnp.float32),
             pltpu.VMEM((members,) + cut, jnp.float32),
@@ -380,27 +426,54 @@
             pltpu.VMEM((members,) + cut, jnp.float32),
             pltpu.VMEM(cut, jnp.float32),
             pltpu.VMEM(jacobian.shape, jnp.bfloat16),
+            pltpu.VMEM(obs_value.shape, jnp.bfloat16),
+            pltpu.VMEM(obs_weight.shape, jnp.bfloat16),
+            pltpu.VMEM(channel_mask.shape, jnp.int32),
+            pltpu.SMEM(obs_cell.shape, jnp.int32),
+            pltpu.SMEM(obs_count.shape, jnp.int32),
             pltpu.VMEM((every, LANES), jnp.int32),
+            pltpu.VMEM((slots, channels), jnp.float32),
             pltpu.VMEM((STEPS + 1, every, cells_y), jnp.float32),
             pltpu.VMEM((cells_x, 2 * LANES, cells_y), jnp.bfloat16),
             pltpu.VMEM((cells_x, LANES, cells_y), jnp.bfloat16),
             pltpu.VMEM((cells_x, 3 * every, cells_y), jnp.bfloat16),
-            pltpu.VMEM((every, 2 * LANES), jnp.float32),
-            pltpu.VMEM((cols, slots, 2 * LANES), jnp.float32),
+            pltpu.VMEM((every, LANES), jnp.float32),
+            pltpu.VMEM((cols, slots + max(8, slots // cols), LANES), jnp.float32),
+            pltpu.VMEM((cols, slots + max(8, slots // cols), LANES), jnp.float32),
             pltpu.VMEM((levs, slots, LANES), jnp.float32),
             pltpu.VMEM((every, LANES), jnp.float32),
-            pltpu.SemaphoreType.DMA((2 + (members + 2) * cut[0],)),
-            pltpu.SemaphoreType.DMA(((members + 1) * cut[0],)),
+            pltpu.SemaphoreType.DMA((7 + (members + 2) * cut[0],)),
+            pltpu.SemaphoreType.DMA((3,)),
             pltpu.SemaphoreType.DMA((4, max(cols, levs))),
             pltpu.SemaphoreType.DMA((4, max(cols, levs))),
         ],
         compiler_params=pltpu.CompilerParams(
-            collective_id=0, has_side_effects=True, vmem_limit_bytes=32 * 1024 * 1024
+            collective_id=0, has_side_effects=True, vmem_limit_bytes=63 * 1024 * 1024
         ),
     )(
         control.reshape(flat), control_ens.reshape((members,) + flat), ensemble, spread.reshape(flat),
         jacobian, obs_value, obs_weight, channel_mask, obs_cell, obs_count,
     )
+    out_control, out_ens, departures = pl.pallas_call(
+        functools.partial(adjoint, (levels, cells_x, cells_y)),
+        out_shape=(
+            jax.ShapeDtypeStruct(flat, jnp.float32),
+            jax.ShapeDtypeStruct((members,) + flat, jnp.float32),
+            jax.ShapeDtypeStruct((slots, channels), jnp.float32),
+        ),
+        in_specs=[hbm] * 5,
+        out_specs=(hbm,) * 3,
+        scratch_shapes=[
+            pltpu.VMEM(cut, jnp.float32),
+            pltpu.VMEM((members,) + cut, jnp.float32),
+            pltpu.VMEM((cells_x, 3 * every, cells_y), jnp.bfloat16),
+            pltpu.VMEM((every, LANES), jnp.float32),
+            pltpu.VMEM((slots, channels), jnp.float32),
+            pltpu.SemaphoreType.DMA((3 + (members + 1) * cut[0],)),
+            pltpu.SemaphoreType.DMA((1 + (members + 1) * cut[0],)),
+        ],
+        compiler_params=pltpu.CompilerParams(vmem_limit_bytes=63 * 1024 * 1024),
+    )(control.reshape(flat), control_ens.reshape((members,) + flat), weights, amount, held)
     return out_control.reshape(control.shape), out_ens.reshape(control_ens.shape), departures
 
 

time: 31.5 us -> 24 us (0.76)
  local copies, waits for them, and re-layouts: 8.94 us -> 0 us
  Pallas kernels: 21.5 us -> 23.2 us
    unnamed x23 -> x0, local copies, waits for them, and re-layouts: 8.94 us -> none
    pallas_call x0 -> x1, Pallas kernels: none -> 2.69 us  [local_fused(): pl.pallas_call(functools.partial(adjoint, (levels, cells_x, cells_y)), ou...]
    pallas_call x1, Pallas kernels: 21.5 us -> 20.5 us  [local_fused(): pl.pallas_call(functools.partial(fused, (cols, levs, slots, levels, cells...]
where the time goes in v2:
time: 24 us; the launch traced here: 23.9 us
  Pallas kernels  23.2 us (97%)
  between operations  0.64 us (3%)
    pallas_call x1, Pallas kernels, local_fused(): pl.pallas_call(functools.partial(fused, (cols, levs, slots, levels, cells...  20.5 us
    pallas_call x1, Pallas kernels, local_fused(): pl.pallas_call(functools.partial(adjoint, (levels, cells_x, cells_y)), ou...  2.69 us

profile of v2, /device:TPU:0, one launch (start us, length us, event | category | flops | bytes accessed | tf_op | source)
XLA Modules:
  0.0 23.9 jit_solution(2304041780145894959)
XLA Ops:
  0.6 20.5 %shard_map.121 = (bf16[8,192,256]{2,1,0:T(8,128)(2,1)}, f32[64,128]{1,0:T(8,128)}, f32[16,128]{1,0:T(8,128)}) custom-call(f32[256,256]{1,0:T(8,128)} %bitcast.7, f32[2,256,256]{2,1,0:T(8,128)} %bitcast.5, bf16[2,32,8,256]{3,2,1,0:T(8,128)(2,1)} %ens_hbm.1, f32[256,256]{1,0:T(8,128)} %bitcast.9, bf16[16,32,128]{2,1,0:T(8,128)(2,1)} %jac_hbm.1, ...), custom_call_target="tpu_custom_call" | custom-call | tf_op jit(solution)/shard_map/pallas_call | solution.py:413
  21.2 2.7 %shard_map.122 = (f32[256,256]{1,0:T(8,128)}, f32[2,256,256]{2,1,0:T(8,128)}, f32[16,128]{1,0:T(8,128)}) custom-call(f32[256,256]{1,0:T(8,128)} %bitcast.8, f32[2,256,256]{2,1,0:T(8,128)} %bitcast.6, bf16[8,192,256]{2,1,0:T(8,128)(2,1)} %get-tuple-element.9.wst_hbm, f32[64,128]{1,0:T(8,128)} %get-tuple-element.10.a_hbm, f32[16,128]{1,0:T(8,128)} %get-tuple-element.11.dep_hbm), custom_call_target="tpu_custom_call" | custom-call | tf_op jit(solution)/shard_map/pallas_call | solution.py:457

commit v3 on v2

--- a/solution.py
+++ b/solution.py
@@ -138,7 +138,7 @@
     cfg,
     ctl_hbm, cen_hbm, ens_hbm, spr_hbm, jac_hbm, val_hbm, wgt_hbm, msk_hbm, cell_hbm, count_hbm,
     wst_hbm, a_hbm, dep_hbm,
-    ctl, cen, ens, ensf, spr, jac, val_ref, wgt_ref, msk_ref, cell_ref, count_ref, cells, dep_ref, ey, fst, vst, wst, found_ref, pv, pv_in, rad_in, a_all,
+    ctl, cen, ens, ensf, spr, jac, val_ref, wgt_ref, msk_ref, cell_ref, count_ref, cells, dep_ref, ey, fst, vst, wst, pv, pv_in, dep_in, a_out, a_in, a_all,
     in_sem, out_sem, send_sem, recv_sem,
 ):
     cols, levs, slots, lev, cx, ny = cfg
@@ -147,7 +147,6 @@
     every = cols * slots
     me, my_lev = lax.axis_index("col"), lax.axis_index("lev")
     table = stencil_power()
-    parts = slots // max(8, cap)
 
     halves = range(ny // LANES)
     lanes_of = [slice(h * LANES, (h + 1) * LANES) for h in halves]
@@ -156,33 +155,34 @@
     fields = len(pairs)
     pairs += [(ens_hbm, ens)] + [(spr_hbm.at[:, lanes_of[h]], spr.at[h]) for h in halves]
     small = len(pairs)
-    pairs += [(jac_hbm, jac), (val_hbm, val_ref), (wgt_hbm, wgt_ref), (msk_hbm, msk_ref), (count_hbm, count_ref)]
+    pairs += [(jac_hbm.at[pl.ds(my_lev * (slots // levs), slots // levs)], jac.at[my_lev]), (val_hbm, val_ref), (wgt_hbm, wgt_ref), (msk_hbm, msk_ref), (count_hbm, count_ref)]
     pairs += [(cell_hbm, cell_ref)]
     loads = [pltpu.make_async_copy(src, dst, in_sem.at[i]) for i, (src, dst) in enumerate(pairs)]
     loads[-1].start()
     barrier = pltpu.get_barrier_semaphore()
-    for d in range(1, cols):
+    peers = cols * levs
+    my_id = me * levs + my_lev
+    for d in range(1, peers):
+        to = lax.rem(my_id + d, peers)
         pl.semaphore_signal(
-            barrier, inc=1, device_id={"col": lax.rem(me + d, cols)}, device_id_type=pl.DeviceIdType.MESH
+            barrier, inc=1, device_id={"col": lax.div(to, levs), "lev": lax.rem(to, levs)},
+            device_id_type=pl.DeviceIdType.MESH,
         )
-    for d in range(1, levs):
-        pl.semaphore_signal(
-            barrier, inc=1, device_id={"lev": lax.rem(my_lev + d, levs)}, device_id_type=pl.DeviceIdType.MESH
-        )
-
     for load in loads[:-1]:
         load.start()
 
-    def send(phase, axis, peers, mine, src_of, dst):
+    def send(phase, axis, src_of, dst):
+        count, mine = {"col": (cols, me), "lev": (levs, my_lev), "all": (peers, my_id)}[axis]
         copies = []
-        for d in range(1, peers):
-            to = lax.rem(mine + d, peers)
+        for d in range(1, count):
+            to = lax.rem(mine + d, count)
+            device = {"col": lax.div(to, levs), "lev": lax.rem(to, levs)} if axis == "all" else {axis: to}
             copy = pltpu.make_async_remote_copy(
                 src_ref=src_of(to),
                 dst_ref=dst,
                 send_sem=send_sem.at[phase, d],
                 recv_sem=recv_sem.at[phase, d],
-                device_id={axis: to},
+                device_id=device,
                 device_id_type=pl.DeviceIdType.MESH,
             )
             copy.start()
@@ -197,8 +197,10 @@
         own = jnp.where(row == r, cell_ref[r], own)
     my_rows = pl.ds(pl.multiple_of(me * slots, slots), slots)
     cells[my_rows, :] = own
-    pl.semaphore_wait(barrier, cols + levs - 2)
-    cell_copies = send(0, "col", cols, me, lambda to: cells.at[my_rows], cells.at[my_rows])
+    pl.semaphore_wait(barrier, peers - 1)
+    cell_copies = send(0, "col", lambda to: cells.at[my_rows], cells.at[my_rows])
+    share = slots // levs
+    jac_copies = send(2, "lev", lambda to: jac_hbm.at[pl.ds(to * share, share)], jac.at[my_lev])
 
     for load in loads[:fields]:
         load.wait()
@@ -281,66 +283,68 @@
     sums = sums[0:every, 0:LANES] + sums[0:every, LANES:] + sums[every:, 0:LANES]
     group = lax.shift_right_logical(y_lane, jnp.full_like(y_lane, lev.bit_length() - 1))
     found = jnp.where(group == 0, found + pltpu.roll(found, lev, 1), found * (1.0 / math.sqrt(2)))
-    found_ref[...] = jnp.where(group == 3, 0.0, found)
-    window = slots // parts
-    for s in range(cols):
-        pv[s, 0:slots, :] = sums[s * slots : (s + 1) * slots]
-        start = s * slots + lax.div(me * cap, window) * window
-        pv[s, slots:, :] = found_ref[pl.ds(pl.multiple_of(start, window), window), :]
-    pv_in[me] = pv[me]
-    copies = send(1, "col", cols, me, lambda to: pv.at[to], pv_in.at[me])
+    found = jnp.where(group == 3, 0.0, found)
+    for q in range(peers):
+        pv[q, 0:share, :] = sums[q * share : (q + 1) * share]
+        pv[q, share:, :] = found[q * share : (q + 1) * share]
+    pv_in[my_id] = pv[my_id]
+    copies = send(1, "all", lambda to: pv.at[to], pv_in.at[my_id])
     for load in loads[small:-1]:
         load.wait()
-    for copy in copies:
+    for copy in jac_copies + copies:
         copy.wait()
 
-    fields_at = pv_in[0, 0:slots, :]
-    for s in range(1, cols):
-        fields_at = fields_at + pv_in[s, 0:slots, :]
-    per_part = cols // parts
-    pieces = []
-    for p in range(parts):
-        piece = pv_in[p * per_part, slots:, :]
-        for s in range(p * per_part + 1, (p + 1) * per_part):
-            piece = piece + pv_in[s, slots:, :]
-        pieces.append(piece)
-    values = jnp.concatenate(pieces, axis=0) if parts > 1 else pieces[0]
-    columns = spread_groups(fields_at * values, lev)
+    row = lax.broadcasted_iota(jnp.int32, (2 * share, LANES), 0)
+    lane = lax.broadcasted_iota(jnp.int32, (2 * share, LANES), 1)
+    own_lane = lax.shift_right_logical(lane, jnp.full_like(lane, lev.bit_length() - 1)) == (row & (share - 1))
+    values, blocks = [], []
+    for j in range(levs):
+        both = pv_in[j]
+        for s in range(1, cols):
+            both = both + pv_in[s * levs + j]
+        turned = pltpu.roll(both, share, 0)
+        values.append(jnp.where(row < share, turned, both))
+        blocks.append(jnp.where(own_lane, spread_groups(both * turned, lev), 0.0))
     jac_rows = jac[...].reshape(slots * lev, LANES)
-    per = LANES // lev
-    lane_group = lax.shift_right_logical(lane, jnp.full_like(lane, lev.bit_length() - 1))
-    tiles = slots // per
-    block = jnp.concatenate(
-        [jnp.where(row == q * per + lane_group, columns, 0.0) for q in range(tiles)], axis=1
-    ).astype(jnp.bfloat16)
-    rad_in[my_lev] = dot(block, jac_rows, 0)
-    for copy in send(2, "lev", levs, my_lev, lambda to: rad_in.at[my_lev], rad_in.at[my_lev]):
+    block = jnp.concatenate([jnp.concatenate(blocks, axis=1)] * 2, axis=0).astype(jnp.bfloat16)
+    radiance = dot(block, jac_rows, 0)[0 : 2 * share]
+
+    slot_in = my_lev * share + (row & (share - 1))
+    filled = jnp.zeros((2 * share, LANES), jnp.bool_)
+    for t in range(cols):
+        filled = filled | ((slot_in >= t * cap) & (slot_in < t * cap + jnp.minimum(count_ref[0, t], cap)))
+
+    def mine(ref):
+        whole = ref[...].astype(jnp.float32)
+        part = whole[0:share]
+        for j in range(1, levs):
+            part = jnp.where(my_lev == j, whole[j * share : (j + 1) * share], part)
+        return jnp.concatenate([part, part], axis=0)
+
+    departure = jnp.where(
+        filled & (mine(msk_ref) > 0.0), mine(wgt_ref) * (radiance - mine(val_ref)), 0.0
+    )
+    dep_in[my_lev] = departure
+    dep_copies = send(4, "lev", lambda to: dep_in.at[my_lev], dep_in.at[my_lev])
+    doubled = jnp.concatenate([departure, departure], axis=0).astype(jnp.bfloat16)
+    spread_out = dot(doubled, jac_rows, 1)[0 : 2 * share]
+    half = (row >= share) == ((my_lev & 1) == 1)
+    for j in range(levs):
+        part = jnp.where(own_lane, spread_out[:, j * LANES : (j + 1) * LANES], 0.0)
+        amount = spread_groups(part, lev) * values[j]
+        a_out[j] = jnp.where(half, amount, 0.0)
+    a_in[my_id] = a_out[my_lev]
+    a_copies = send(3, "all", lambda to: a_out.at[lax.rem(to, levs)], a_in.at[my_id])
+    for copy in dep_copies:
         copy.wait()
-    radiance = rad_in[0]
-    for s in range(1, levs):
-        radiance = radiance + rad_in[s]
-
-    filled = jnp.zeros((slots, LANES), jnp.bool_)
-    for t in range(cols):
-        filled = filled | ((row >= t * cap) & (row < t * cap + jnp.minimum(count_ref[0, t], cap)))
-    departure = jnp.where(
-        filled & (msk_ref[...] > 0),
-        wgt_ref[...].astype(jnp.float32) * (radiance - val_ref[...].astype(jnp.float32)),
-        0.0,
-    )
-    dep_ref[...] = departure
+    for j in range(levs):
+        dep_ref[j * share : (j + 1) * share, :] = dep_in[j, 0:share, :]
     dep_store = pltpu.make_async_copy(dep_ref, dep_hbm, out_sem.at[out_sem.shape[0] - 1])
     dep_store.start()
-    spread_out = dot(departure.astype(jnp.bfloat16), jac_rows, 1)
-    increment = jnp.zeros((slots, LANES), jnp.float32)
-    for q in range(tiles):
-        part = spread_out[:, q * LANES : (q + 1) * LANES]
-        increment = increment + jnp.where(row == q * per + lane_group, part, 0.0)
-    increment = spread_groups(increment, lev)
-    a_all[my_rows, :] = increment * values
-    for copy in send(3, "col", cols, me, lambda to: a_all.at[my_rows], a_all.at[my_rows]):
+    for copy in a_copies:
         copy.wait()
-
+    for q in range(peers // 2):
+        a_all[q * 2 * share : (q + 1) * 2 * share, :] = a_in[2 * q] + a_in[2 * q + 1]
     a_store = pltpu.make_async_copy(a_all, a_hbm, out_sem.at[1])
     a_store.start()
     for store in (wst_store, a_store, dep_store):
@@ -390,14 +394,14 @@
         store.wait()
 
 
-def fits(members, levels, cells_x, cells_y, slot_total, channels, peers):
+def fits(members, levels, cells_x, cells_y, slot_total, channels, peers, level_blocks):
     def power(n):
         return n & (n - 1) == 0
     return (
         members == 2 and levels * 4 == LANES and channels == LANES and cells_x == 8
         and cells_y % LANES == 0 and power(cells_y) and cells_y <= 256 and power(peers) and slot_total % 16 == 0
         and power(slot_total // peers) and peers * slot_total * 3 <= 256
-        and peers * cells_x > 2 * STEPS
+        and peers * cells_x > 2 * STEPS and slot_total == 4 * level_blocks and level_blocks == 4
     )
 
 
@@ -406,7 +410,7 @@
     levels, cells_x, cells_y = control.shape
     slots, _, channels = jacobian.shape
     cols, levs = lax.axis_size("col"), lax.axis_size("lev")
-    every = cols * slots
+    every, peers, share = cols * slots, cols * levs, slots // levs
     flat = (levels * cells_x, cells_y)
     cut = (cells_y // LANES, levels * cells_x, LANES)
     hbm = pl.BlockSpec(memory_space=pltpu.HBM)
@@ -425,7 +429,7 @@
             pltpu.VMEM(ensemble.shape, jnp.bfloat16),
             pltpu.VMEM((members,) + cut, jnp.float32),
             pltpu.VMEM(cut, jnp.float32),
-            pltpu.VMEM(jacobian.shape, jnp.bfloat16),
+            pltpu.VMEM((levs, share) + jacobian.shape[1:], jnp.bfloat16),
             pltpu.VMEM(obs_value.shape, jnp.bfloat16),
             pltpu.VMEM(obs_weight.shape, jnp.bfloat16),
             pltpu.VMEM(channel_mask.shape, jnp.int32),
@@ -437,15 +441,16 @@
             pltpu.VMEM((cells_x, 2 * LANES, cells_y), jnp.bfloat16),
             pltpu.VMEM((cells_x, LANES, cells_y), jnp.bfloat16),
             pltpu.VMEM((cells_x, 3 * every, cells_y), jnp.bfloat16),
-            pltpu.VMEM((every, LANES), jnp.float32),
-            pltpu.VMEM((cols, slots + max(8, slots // cols), LANES), jnp.float32),
-            pltpu.VMEM((cols, slots + max(8, slots // cols), LANES), jnp.float32),
-            pltpu.VMEM((levs, slots, LANES), jnp.float32),
+            pltpu.VMEM((peers, 2 * share, LANES), jnp.float32),
+            pltpu.VMEM((peers, 2 * share, LANES), jnp.float32),
+            pltpu.VMEM((levs, 2 * share, LANES), jnp.float32),
+            pltpu.VMEM((levs, 2 * share, LANES), jnp.float32),
+            pltpu.VMEM((peers, 2 * share, LANES), jnp.float32),
             pltpu.VMEM((every, LANES), jnp.float32),
             pltpu.SemaphoreType.DMA((7 + (members + 2) * cut[0],)),
             pltpu.SemaphoreType.DMA((3,)),
-            pltpu.SemaphoreType.DMA((4, max(cols, levs))),
-            pltpu.SemaphoreType.DMA((4, max(cols, levs))),
+            pltpu.SemaphoreType.DMA((5, peers)),
+            pltpu.SemaphoreType.DMA((5, peers)),
         ],
         compiler_params=pltpu.CompilerParams(
             collective_id=0, has_side_effects=True, vmem_limit_bytes=63 * 1024 * 1024
@@ -478,7 +483,7 @@
 
 
 def pick_local(control, control_ens, ensemble, spread, jacobian, *obs):
-    sizes = (control_ens.shape[0],) + control.shape + (jacobian.shape[0], jacobian.shape[2], lax.axis_size("col"))
+    sizes = (control_ens.shape[0],) + control.shape + (jacobian.shape[0], jacobian.shape[2], lax.axis_size("col"), lax.axis_size("lev"))
     run = local_fused if fits(*sizes) else local
     return run(control, control_ens, ensemble, spread, jacobian, *obs)
 

time: 24 us -> 23.9 us (level)
  no operation moved by 1% of the time
where the time goes in v3:
time: 23.9 us; the launch traced here: 23.8 us
  Pallas kernels  23.1 us (97%)
  between operations  0.64 us (3%)
    pallas_call x1, Pallas kernels, local_fused(): pl.pallas_call(functools.partial(fused, (cols, levs, slots, levels, cells...  20.4 us
    pallas_call x1, Pallas kernels, local_fused(): pl.pallas_call(functools.partial(adjoint, (levels, cells_x, cells_y)), ou...  2.69 us

profile of v3, /device:TPU:0, one launch (start us, length us, event | category | flops | bytes accessed | tf_op | source)
XLA Modules:
  0.0 23.8 jit_solution(12514339395053012061)
XLA Ops:
  0.6 20.4 %shard_map.121 = (bf16[8,192,256]{2,1,0:T(8,128)(2,1)}, f32[64,128]{1,0:T(8,128)}, f32[16,128]{1,0:T(8,128)}) custom-call(f32[256,256]{1,0:T(8,128)} %bitcast.7, f32[2,256,256]{2,1,0:T(8,128)} %bitcast.5, bf16[2,32,8,256]{3,2,1,0:T(8,128)(2,1)} %ens_hbm.1, f32[256,256]{1,0:T(8,128)} %bitcast.9, bf16[16,32,128]{2,1,0:T(8,128)(2,1)} %jac_hbm.1, ...), custom_call_target="tpu_custom_call" | custom-call | tf_op jit(solution)/shard_map/pallas_call | solution.py:417
  21.1 2.7 %shard_map.122 = (f32[256,256]{1,0:T(8,128)}, f32[2,256,256]{2,1,0:T(8,128)}, f32[16,128]{1,0:T(8,128)}) custom-call(f32[256,256]{1,0:T(8,128)} %bitcast.8, f32[2,256,256]{2,1,0:T(8,128)} %bitcast.6, bf16[8,192,256]{2,1,0:T(8,128)(2,1)} %get-tuple-element.9.wst_hbm, f32[64,128]{1,0:T(8,128)} %get-tuple-element.10.a_hbm, f32[16,128]{1,0:T(8,128)} %get-tuple-element.11.dep_hbm), custom_call_target="tpu_custom_call" | custom-call | tf_op jit(solution)/shard_map/pallas_call | solution.py:462

commit v4 on v3

--- a/solution.py
+++ b/solution.py
@@ -162,12 +162,11 @@
     barrier = pltpu.get_barrier_semaphore()
     peers = cols * levs
     my_id = me * levs + my_lev
-    for d in range(1, peers):
-        to = lax.rem(my_id + d, peers)
-        pl.semaphore_signal(
-            barrier, inc=1, device_id={"col": lax.div(to, levs), "lev": lax.rem(to, levs)},
-            device_id_type=pl.DeviceIdType.MESH,
-        )
+    for axis, count, mine in (("col", cols, me), ("lev", levs, my_lev)):
+        for d in range(1, count):
+            pl.semaphore_signal(
+                barrier, inc=1, device_id={axis: lax.rem(mine + d, count)}, device_id_type=pl.DeviceIdType.MESH
+            )
     for load in loads[:-1]:
         load.start()
 
@@ -197,7 +196,7 @@
         own = jnp.where(row == r, cell_ref[r], own)
     my_rows = pl.ds(pl.multiple_of(me * slots, slots), slots)
     cells[my_rows, :] = own
-    pl.semaphore_wait(barrier, peers - 1)
+    pl.semaphore_wait(barrier, cols + levs - 2)
     cell_copies = send(0, "col", lambda to: cells.at[my_rows], cells.at[my_rows])
     share = slots // levs
     jac_copies = send(2, "lev", lambda to: jac_hbm.at[pl.ds(to * share, share)], jac.at[my_lev])

time: 23.9 us -> 23.7 us (level)
    pallas_call x1, Pallas kernels: 20.4 us -> 20.2 us  [local_fused(): pl.pallas_call(functools.partial(fused, (cols, levs, slots, levels, cells...]
where the time goes in v4:
time: 23.7 us; the launch traced here: 23.5 us
  Pallas kernels  22.9 us (97%)
  between operations  0.64 us (3%)
    pallas_call x1, Pallas kernels, local_fused(): pl.pallas_call(functools.partial(fused, (cols, levs, slots, levels, cells...  20.2 us
    pallas_call x1, Pallas kernels, local_fused(): pl.pallas_call(functools.partial(adjoint, (levels, cells_x, cells_y)), ou...  2.69 us

profile of v4, /device:TPU:0, one launch (start us, length us, event | category | flops | bytes accessed | tf_op | source)
XLA Modules:
  0.0 23.5 jit_solution(16956708516261934119)
XLA Ops:
  0.6 20.2 %shard_map.121 = (bf16[8,192,256]{2,1,0:T(8,128)(2,1)}, f32[64,128]{1,0:T(8,128)}, f32[16,128]{1,0:T(8,128)}) custom-call(f32[256,256]{1,0:T(8,128)} %bitcast.7, f32[2,256,256]{2,1,0:T(8,128)} %bitcast.5, bf16[2,32,8,256]{3,2,1,0:T(8,128)(2,1)} %ens_hbm.1, f32[256,256]{1,0:T(8,128)} %bitcast.9, bf16[16,32,128]{2,1,0:T(8,128)(2,1)} %jac_hbm.1, ...), custom_call_target="tpu_custom_call" | custom-call | tf_op jit(solution)/shard_map/pallas_call | solution.py:416
  20.8 2.7 %shard_map.122 = (f32[256,256]{1,0:T(8,128)}, f32[2,256,256]{2,1,0:T(8,128)}, f32[16,128]{1,0:T(8,128)}) custom-call(f32[256,256]{1,0:T(8,128)} %bitcast.8, f32[2,256,256]{2,1,0:T(8,128)} %bitcast.6, bf16[8,192,256]{2,1,0:T(8,128)(2,1)} %get-tuple-element.9.wst_hbm, f32[64,128]{1,0:T(8,128)} %get-tuple-element.10.a_hbm, f32[16,128]{1,0:T(8,128)} %get-tuple-element.11.dep_hbm), custom_call_target="tpu_custom_call" | custom-call | tf_op jit(solution)/shard_map/pallas_call | solution.py:461

commit v5 on v4

--- a/solution.py
+++ b/solution.py
@@ -189,12 +189,13 @@
         return copies
 
     loads[-1].wait()
-    row = lax.broadcasted_iota(jnp.int32, (slots, LANES), 0)
-    lane = lax.broadcasted_iota(jnp.int32, (slots, LANES), 1)
-    own = jnp.zeros((slots, LANES), jnp.int32)
-    for r in range(slots):
-        own = jnp.where(row == r, cell_ref[r], own)
-    my_rows = pl.ds(pl.multiple_of(me * slots, slots), slots)
+    pack = slots // 2
+    row = lax.broadcasted_iota(jnp.int32, (pack, LANES), 0)
+    first = lax.broadcasted_iota(jnp.int32, (pack, LANES), 1) < LANES // 2
+    own = jnp.zeros((pack, LANES), jnp.int32)
+    for r in range(pack):
+        own = jnp.where(row == r, jnp.where(first, cell_ref[r], cell_ref[pack + r]), own)
+    my_rows = pl.ds(pl.multiple_of(me * pack, pack), pack)
     cells[my_rows, :] = own
     pl.semaphore_wait(barrier, cols + levs - 2)
     cell_copies = send(0, "col", lambda to: cells.at[my_rows], cells.at[my_rows])
@@ -230,7 +231,12 @@
     for copy in cell_copies:
         copy.wait()
 
-    cell = cells[...]
+    rows_of = []
+    for s in range(cols):
+        packed = cells[s * pack : (s + 1) * pack, :]
+        turned = pltpu.roll(packed, LANES // 2, 1)
+        rows_of += [jnp.where(first, packed, turned), jnp.where(first, turned, packed)]
+    cell = jnp.concatenate(rows_of, axis=0)
     shift = ny.bit_length() - 1
     cell_x = lax.shift_right_logical(cell, jnp.full_like(cell, shift))
     cell_y = cell & (ny - 1)
@@ -434,7 +440,7 @@
             pltpu.VMEM(channel_mask.shape, jnp.int32),
             pltpu.SMEM(obs_cell.shape, jnp.int32),
             pltpu.SMEM(obs_count.shape, jnp.int32),
-            pltpu.VMEM((every, LANES), jnp.int32),
+            pltpu.VMEM((every // 2, LANES), jnp.int32),
             pltpu.VMEM((slots, channels), jnp.float32),
             pltpu.VMEM((STEPS + 1, every, cells_y), jnp.float32),
             pltpu.VMEM((cells_x, 2 * LANES, cells_y), jnp.bfloat16),

time: 23.7 us -> 23.7 us (level)
  no operation moved by 1% of the time
where the time goes in v5:
time: 23.7 us; the launch traced here: 23.5 us
  Pallas kernels  22.9 us (97%)
  between operations  0.64 us (3%)
    pallas_call x1, Pallas kernels, local_fused(): pl.pallas_call(functools.partial(fused, (cols, levs, slots, levels, cells...  20.2 us
    pallas_call x1, Pallas kernels, local_fused(): pl.pallas_call(functools.partial(adjoint, (levels, cells_x, cells_y)), ou...  2.68 us

profile of v5, /device:TPU:0, one launch (start us, length us, event | category | flops | bytes accessed | tf_op | source)
XLA Modules:
  0.0 23.5 jit_solution(5023770496655255726)
XLA Ops:
  0.6 20.2 %shard_map.121 = (bf16[8,192,256]{2,1,0:T(8,128)(2,1)}, f32[64,128]{1,0:T(8,128)}, f32[16,128]{1,0:T(8,128)}) custom-call(f32[256,256]{1,0:T(8,128)} %bitcast.7, f32[2,256,256]{2,1,0:T(8,128)} %bitcast.5, bf16[2,32,8,256]{3,2,1,0:T(8,128)(2,1)} %ens_hbm.1, f32[256,256]{1,0:T(8,128)} %bitcast.9, bf16[16,32,128]{2,1,0:T(8,128)(2,1)} %jac_hbm.1, ...), custom_call_target="tpu_custom_call" | custom-call | tf_op jit(solution)/shard_map/pallas_call | solution.py:422
  20.8 2.7 %shard_map.122 = (f32[256,256]{1,0:T(8,128)}, f32[2,256,256]{2,1,0:T(8,128)}, f32[16,128]{1,0:T(8,128)}) custom-call(f32[256,256]{1,0:T(8,128)} %bitcast.8, f32[2,256,256]{2,1,0:T(8,128)} %bitcast.6, bf16[8,192,256]{2,1,0:T(8,128)(2,1)} %get-tuple-element.9.wst_hbm, f32[64,128]{1,0:T(8,128)} %get-tuple-element.10.a_hbm, f32[16,128]{1,0:T(8,128)} %get-tuple-element.11.dep_hbm), custom_call_target="tpu_custom_call" | custom-call | tf_op jit(solution)/shard_map/pallas_call | solution.py:467
